TPU v7x, 32 devices: a whole 2x2x4 slice. The times are simulated.
32 devices in a mesh: dp: 4 (over y, core), seq: 8 (over z, x).
Axes of the slice: x: 2, y: 2, z: 4, core: 2. Of those that a mesh axis runs over, the one named last changes fastest.
Arguments:
- inputs: bfloat16 [16, 1024, 768], P('dp', 'seq'), may hold values from -6 to 6
- cotangent: bfloat16 [16, 1024, 768], P('dp', 'seq'), may hold values from -6 to 6
- lengths: int32 [16, 4], P('dp'), may hold values from 0 to 1024, as said below
- clusters: int32 [16, 1024, 12], P('dp', 'seq'), may hold values from 0 to 99, as said below
- gain_attn: float32 [768], replicated, may hold values from 0.1 to 1.9
- bias_attn: float32 [768], replicated, may hold values from -0.6 to 0.6
- w_query: bfloat16 [768, 768], replicated, may hold values from -1 to 1
- w_key: bfloat16 [768, 768], replicated, may hold values from -0.3125 to 0.3125
- w_value: bfloat16 [768, 768], replicated, may hold values from -0.21875 to 0.21875
- w_out: bfloat16 [768, 768], replicated, may hold values from -0.875 to 0.875
- gain_ffn: float32 [768], replicated, may hold values from 0.1 to 1.9
- bias_ffn: float32 [768], replicated, may hold values from -1.8 to 1.8
- w_up: bfloat16 [768, 3072], replicated, may hold values from -0.21875 to 0.21875
- w_down: bfloat16 [3072, 768], replicated, may hold values from -0.109375 to 0.109375
Outputs:
- output: float32 [16, 1024, 768], P('dp', 'seq')
- grad_inputs: float32 [16, 1024, 768], P('dp', 'seq')
- grad_gain_attn: float32 [768], P('seq')
- grad_bias_attn: float32 [768], P('seq')
- grad_w_query: float32 [768, 768], P('seq')
- grad_w_key: float32 [768, 768], P('seq')
- grad_w_value: float32 [768, 768], P('seq')
- grad_w_out: float32 [768, 768], P('seq')
- grad_gain_ffn: float32 [768], P('seq')
- grad_bias_ffn: float32 [768], P('seq')
- grad_w_up: float32 [768, 3072], P('seq')
- grad_w_down: float32 [3072, 768], P('seq')
Inputs may be any that keep to these rules, and one draw needn't show every extreme that they name: Each row's lengths add up to 1024; a length may be 0. In every aligned block of 4 rows one row is a single document of 1024 tokens. `clusters`: in every row and head each of the 100 cluster numbers is given to at least one token.
All inputs are finite; a program needn't handle non-finite values.
Results may differ from a plain program's by a relative error of at most 0.018.
Values may be sent and summed in bfloat16 or wider, within the bound.
A program may use at most 192 MiB of HBM per device.

v0:
```python
import jax
import jax.numpy as jnp
from jax import lax
from jax.sharding import PartitionSpec as P

CLUSTERS = 100


EPSILON = 1e-05
PRECISE = lax.Precision.HIGHEST


def norm_forward(values, gain, bias):
    average = jnp.mean(values, axis=-1, keepdims=True)
    centered = values - average
    inverse = lax.rsqrt(jnp.mean(centered * centered, axis=-1, keepdims=True) + EPSILON)
    unit = centered * inverse
    return (unit * gain + bias, unit, inverse)


def norm_backward(grad, unit, inverse, gain):
    scaled = grad * gain
    inner = (
        scaled
        - jnp.mean(scaled, axis=-1, keepdims=True)
        - unit * jnp.mean(scaled * unit, axis=-1, keepdims=True)
    )
    return (inner * inverse, jnp.sum(grad * unit, axis=0), jnp.sum(grad, axis=0))


def inner_rows(left, right):
    return lax.dot_general(
        left, right, (((0,), (0,)), ((), ())), preferred_element_type=jnp.float32
    )


def times_transpose(left, right):
    return lax.dot_general(
        left, right, (((1,), (1,)), ((), ())), preferred_element_type=jnp.float32
    )


def plain_dot(left, right):
    return jnp.dot(left, right, preferred_element_type=jnp.float32)


def smooth_gelu(values):
    return jax.nn.gelu(values, approximate=True)


def local(
    inputs,
    cotangent,
    lengths,
    clusters,
    gain_attn,
    bias_attn,
    w_query,
    w_key,
    w_value,
    w_out,
    gain_ffn,
    bias_ffn,
    w_up,
    w_down,
):
    row_count, row_tokens, model_width = inputs.shape
    head_count = clusters.shape[2]
    head_dim = model_width // head_count
    doc_count = lengths.shape[1]
    group_count = CLUSTERS
    token_count = row_count * row_tokens
    position = lax.axis_index("seq") * row_tokens + jnp.arange(row_tokens, dtype=jnp.int32)
    doc_ends = jnp.cumsum(lengths, axis=1)
    segment = jnp.sum((position[None, :, None] >= doc_ends[:, None, :]).astype(jnp.int32), axis=2)
    doc_hot = (segment[:, :, None] == jnp.arange(doc_count, dtype=jnp.int32)[None, None, :]).astype(
        jnp.float32
    )
    doc_low = doc_hot.astype(jnp.bfloat16)
    doc_turned = jnp.transpose(doc_hot, (0, 2, 1))
    absent = (lengths == 0).astype(jnp.float32)
    member = (clusters[:, :, :, None] == jnp.arange(group_count, dtype=jnp.int32)).astype(
        jnp.bfloat16
    )
    member_float = member.astype(jnp.float32)
    flat_in = inputs.astype(jnp.float32).reshape(token_count, model_width)
    normed, unit_attn, inv_attn = norm_forward(flat_in, gain_attn, bias_attn)
    normed_low = normed.astype(jnp.bfloat16)
    query_rows = plain_dot(normed_low, w_query).astype(jnp.bfloat16)
    key_rows = plain_dot(normed_low, w_key).astype(jnp.bfloat16)
    value_rows = plain_dot(normed_low, w_value).astype(jnp.bfloat16)
    query_heads = query_rows.reshape(row_count, row_tokens, head_count, head_dim)
    key_heads = key_rows.reshape(row_count, row_tokens, head_count, head_dim)
    value_heads = value_rows.reshape(row_count, row_tokens, head_count, head_dim)
    part_sums = jnp.einsum(
        "rthc,rthd->rhcd", member, query_heads, preferred_element_type=jnp.float32
    )
    part_counts = jnp.sum(member_float, axis=1)
    sums, counts = lax.psum((part_sums, part_counts), "seq")
    centroid = (sums / counts[..., None]).astype(jnp.bfloat16)
    scores = (
        jnp.einsum("rhcd,rthd->rhct", centroid, key_heads, preferred_element_type=jnp.float32)
        * 0.125
    )
    row_max = lax.pmax(jnp.max(scores, axis=3), "seq")
    exp_scores = jnp.exp(scores - row_max[..., None])
    weights = exp_scores.astype(jnp.bfloat16)
    part_denom = jnp.einsum("rhct,rts->rhcs", exp_scores, doc_hot, precision=PRECISE)
    masked = weights[:, :, :, None, :] * jnp.transpose(doc_low, (0, 2, 1))[:, None, None, :, :]
    part_result = jnp.einsum(
        "rhcst,rthd->rhcsd", masked, value_heads, preferred_element_type=jnp.float32
    )
    summed, summed_denom = lax.psum((part_result, part_denom), "seq")
    denom = summed_denom + absent[:, None, None, :]
    result_exact = summed / denom[..., None]
    result = result_exact.astype(jnp.bfloat16).reshape(
        row_count, head_count, group_count, doc_count * head_dim
    )
    picked = jnp.einsum("rthc,rhcx->rthx", member, result, preferred_element_type=jnp.float32)
    picked = picked.reshape(row_count, row_tokens, head_count, doc_count, head_dim)
    attended = (
        jnp.sum(picked * doc_hot[:, :, None, :, None], axis=3)
        .astype(jnp.bfloat16)
        .reshape(token_count, model_width)
    )
    middle = flat_in + plain_dot(attended, w_out)
    normed2, unit_ffn, inv_ffn = norm_forward(middle, gain_ffn, bias_ffn)
    normed2_low = normed2.astype(jnp.bfloat16)
    hidden_pre = plain_dot(normed2_low, w_up)
    active, gelu_back = jax.vjp(smooth_gelu, hidden_pre)
    active_low = active.astype(jnp.bfloat16)
    output = middle + plain_dot(active_low, w_down)
    grad_out = cotangent.reshape(token_count, model_width)
    grad_w_down = inner_rows(active_low, grad_out)
    grad_active = times_transpose(grad_out, w_down)
    grad_pre = gelu_back(grad_active)[0].astype(jnp.bfloat16)
    grad_w_up = inner_rows(normed2_low, grad_pre)
    grad_normed2 = times_transpose(grad_pre, w_up)
    grad_mid_norm, grad_gain_ffn, grad_bias_ffn = norm_backward(
        grad_normed2, unit_ffn, inv_ffn, gain_ffn
    )
    grad_middle = grad_out.astype(jnp.float32) + grad_mid_norm
    grad_branch = grad_middle.astype(jnp.bfloat16)
    grad_w_out = inner_rows(attended, grad_branch)
    grad_att = times_transpose(grad_branch, w_out)
    grad_att = grad_att.reshape(row_count, row_tokens, head_count, 1, head_dim)
    spread = (grad_att * doc_hot[:, :, None, :, None]).reshape(
        row_count, row_tokens, head_count, doc_count * head_dim
    )
    part_grad_result = jnp.einsum("rthc,rthx->rhcx", member_float, spread, precision=PRECISE)
    grad_result = lax.psum(part_grad_result, "seq")
    grad_float = grad_result.reshape(row_count, head_count, group_count, doc_count, head_dim)
    delta = jnp.sum(grad_float * result_exact, axis=4) / denom
    grad_scaled = (grad_float / denom[..., None]).astype(jnp.bfloat16)
    grad_split = jnp.einsum(
        "rhcsd,rthd->rhcst", grad_scaled, value_heads, preferred_element_type=jnp.float32
    )
    grad_prob = jnp.sum(grad_split * doc_turned[:, None, None, :, :], axis=3)
    grad_score = exp_scores * (
        grad_prob - jnp.einsum("rhcs,rts->rhct", delta, doc_hot, precision=PRECISE)
    )
    grad_raw = (grad_score * 0.125).astype(jnp.bfloat16)
    grad_key = jnp.einsum("rhct,rhcd->rthd", grad_raw, centroid, preferred_element_type=jnp.float32)
    grad_key = grad_key.astype(jnp.bfloat16).reshape(token_count, model_width)
    value_split = jnp.einsum(
        "rhct,rhcsd->rthsd", weights, grad_scaled, preferred_element_type=jnp.float32
    )
    grad_value = jnp.sum(value_split * doc_hot[:, :, None, :, None], axis=3)
    grad_value = grad_value.astype(jnp.bfloat16).reshape(token_count, model_width)
    part_grad_cent = jnp.einsum(
        "rhct,rthd->rhcd", grad_raw, key_heads, preferred_element_type=jnp.float32
    )
    grad_cent = lax.psum(part_grad_cent, "seq")
    grad_sums_cent = grad_cent / counts[..., None]
    grad_query = jnp.einsum("rthc,rhcd->rthd", member_float, grad_sums_cent, precision=PRECISE)
    grad_query = grad_query.astype(jnp.bfloat16).reshape(token_count, model_width)
    grad_w_query = inner_rows(normed_low, grad_query)
    grad_w_key = inner_rows(normed_low, grad_key)
    grad_w_value = inner_rows(normed_low, grad_value)
    grad_normed = (
        times_transpose(grad_query, w_query)
        + times_transpose(grad_key, w_key)
        + times_transpose(grad_value, w_value)
    )
    grad_in_norm, grad_gain_attn, grad_bias_attn = norm_backward(
        grad_normed, unit_attn, inv_attn, gain_attn
    )
    grad_inputs = (grad_middle + grad_in_norm).reshape(row_count, row_tokens, model_width)
    shares = (
        lax.psum_scatter(grad_gain_attn, "seq", scatter_dimension=0, tiled=True),
        lax.psum_scatter(grad_bias_attn, "seq", scatter_dimension=0, tiled=True),
        lax.psum_scatter(grad_w_query, "seq", scatter_dimension=0, tiled=True),
        lax.psum_scatter(grad_w_key, "seq", scatter_dimension=0, tiled=True),
        lax.psum_scatter(grad_w_value, "seq", scatter_dimension=0, tiled=True),
        lax.psum_scatter(grad_w_out, "seq", scatter_dimension=0, tiled=True),
        lax.psum_scatter(grad_gain_ffn, "seq", scatter_dimension=0, tiled=True),
        lax.psum_scatter(grad_bias_ffn, "seq", scatter_dimension=0, tiled=True),
        lax.psum_scatter(grad_w_up, "seq", scatter_dimension=0, tiled=True),
        lax.psum_scatter(grad_w_down, "seq", scatter_dimension=0, tiled=True),
    )
    totals = lax.psum(
        (
            shares[0],
            shares[1],
            shares[2],
            shares[3],
            shares[4],
            shares[5],
            shares[6],
            shares[7],
            shares[8],
            shares[9],
        ),
        "dp",
    )
    return (
        output.reshape(row_count, row_tokens, model_width),
        grad_inputs,
        totals[0],
        totals[1],
        totals[2],
        totals[3],
        totals[4],
        totals[5],
        totals[6],
        totals[7],
        totals[8],
        totals[9],
    )


def solution(mesh):
    placed = (
        P("dp", "seq", None),
        P("dp", "seq", None),
        P("dp", None),
        P("dp", "seq", None),
        P(),
        P(),
        P(),
        P(),
        P(),
        P(),
        P(),
        P(),
        P(),
        P(),
    )
    return jax.shard_map(
        local,
        mesh=mesh,
        in_specs=placed,
        out_specs=(
            P("dp", "seq", None),
            P("dp", "seq", None),
            P("seq"),
            P("seq"),
            P("seq", None),
            P("seq", None),
            P("seq", None),
            P("seq", None),
            P("seq"),
            P("seq"),
            P("seq", None),
            P("seq", None),
        ),
        check_vma=False,
    )
```

profile of v0, /device:TPU:0, one launch (start us, length us, event | category | flops | bytes accessed | tf_op | source)
XLA Modules:
  0.0 1438.2 jit_solution(3427418293581253774)
XLA Ops:
  30.1 39.6 %psum.113 = f32[4,12,100]{2,1,0:T(8,128)S(1)} all-reduce(f32[4,12,100]{2,1,0:T(8,128)S(1)} %convert_reduce_fusion), channel_id=1, replica_groups=mesh['dp'=4,'seq'=8] {'seq'}, use_global_device_ids=true, to_apply=%region_4.5 | all-reduce | flops 4800 | bytes 38400 | tf_op jit(solution)/shard_map/psum | solution.py:99
  70.3 39.1 %all-reduce.14.cloned.1.call-done = f32[4,12,100,64]{2,3,1,0:T(8,128)} async-done(((f32[4,12,100,64]{2,3,1,0:T(8,128)}), f32[4,12,100,64]{2,3,1,0:T(8,128)}) %all-reduce.14.cloned.1.call-update) | async-done | bytes 1228816 | tf_op jit(solution)/shard_map/psum | solution.py:99
  113.3 35.5 %pmax.7 = f32[4,12,100]{2,1,0:T(8,128)S(1)} all-reduce(f32[4,12,100]{2,1,0:T(8,128)S(1)} %get-tuple-element.42), channel_id=1, replica_groups=mesh['dp'=4,'seq'=8] {'seq'}, use_global_device_ids=true, to_apply=%region_6.7 | all-reduce | flops 4800 | bytes 38400 | tf_op jit(solution)/shard_map/pmax | solution.py:105
  154.7 6.3 fusion.8
  162.1 7.5 fusion.102
  169.6 204.4 %all-reduce.20.cloned.1.call-done = (f32[4,12,100,4,64]{2,4,3,1,0:T(8,128)}, f32[4,12,100,4]{2,3,1,0:T(4,128)}) async-done(((f32[4,12,100,4,64]{2,4,3,1,0:T(8,128)}, f32[4,12,100,4]{2,3,1,0:T(4,128)}), (f32[4,12,100,4,64]{2,4,3,1,0:T(8,128)}, f32[4,12,100,4]{2,3,1,0:T(4,128)})) %all-reduce.20.cloned.1.call-update) | async-done | bytes 4992016 | tf_op jit(solution)/shard_map/psum | solution.py:113
  384.5 8.8 fusion.6
  404.9 5.1 fusion.13
  410.1 210.3 %all-reduce.16.cloned.1.call-done = f32[4,12,100,4,64]{2,4,3,1,0:T(8,128)} async-done(((f32[4,12,100,4,64]{2,4,3,1,0:T(8,128)}), f32[4,12,100,4,64]{2,4,3,1,0:T(8,128)}) %all-reduce.16.cloned.1.call-update) | async-done | bytes 4915216 | tf_op jit(solution)/shard_map/psum | solution.py:151
  620.4 7.0 multiply_reduce_fusion.1
  647.9 4.3 fusion.7
  656.0 68.5 %all-reduce.18.cloned.1.call-done = f32[4,12,100,64]{2,3,1,0:T(8,128)} async-done(((f32[4,12,100,64]{2,3,1,0:T(8,128)}), f32[4,12,100,64]{2,3,1,0:T(8,128)}) %all-reduce.18.cloned.1.call-update) | async-done | bytes 1228816 | tf_op jit(solution)/shard_map/psum | solution.py:173
  732.1 8.9 fusion.98
  741.0 9.9 fusion.100
  752.8 9.6 convolution_add_fusion
  762.4 34.2 %reduce-scatter.13.cloned.1.call-done = f32[96,768]{1,0:T(8,128)} async-done(((f32[768,768]{1,0:T(8,128)}), f32[96,768]{1,0:T(8,128)}) %reduce-scatter.13.cloned.1.call-update) | async-done | bytes 294928 | tf_op jit(solution)/shard_map/reduce_scatter | solution.py:195
  796.6 71.9 %reduce-scatter.9.cloned.1.call-done = f32[96,768]{1,0:T(8,128)} async-done(((f32[768,768]{1,0:T(8,128)}), f32[96,768]{1,0:T(8,128)}) %reduce-scatter.9.cloned.1.call-update) | async-done | bytes 294928 | tf_op jit(solution)/shard_map/reduce_scatter | solution.py:193
  868.4 72.0 %reduce-scatter.11.cloned.1.call-done = f32[96,768]{1,0:T(8,128)} async-done(((f32[768,768]{1,0:T(8,128)}), f32[96,768]{1,0:T(8,128)}) %reduce-scatter.11.cloned.1.call-update) | async-done | bytes 294928 | tf_op jit(solution)/shard_map/reduce_scatter | solution.py:194
  940.4 72.0 %reduce-scatter.7.cloned.1.call-done = f32[96,768]{1,0:T(8,128)} async-done(((f32[768,768]{1,0:T(8,128)}), f32[96,768]{1,0:T(8,128)}) %reduce-scatter.7.cloned.1.call-update) | async-done | bytes 294928 | tf_op jit(solution)/shard_map/reduce_scatter | solution.py:192
  1012.5 166.4 %reduce-scatter.15.cloned.1.call-done = f32[96,3072]{1,0:T(8,128)} async-done(((f32[768,3072]{1,0:T(8,128)}), f32[96,3072]{1,0:T(8,128)}) %reduce-scatter.15.cloned.1.call-update) | async-done | bytes 1179664 | tf_op jit(solution)/shard_map/reduce_scatter | solution.py:198
  1178.9 166.3 %reduce-scatter.17.cloned.1.call-done = f32[384,768]{1,0:T(8,128)} async-done(((f32[3072,768]{1,0:T(8,128)}), f32[384,768]{1,0:T(8,128)}) %reduce-scatter.17.cloned.1.call-update) | async-done | bytes 1179664 | tf_op jit(solution)/shard_map/reduce_scatter | solution.py:199
  1352.0 35.7 %all-reduce.4 = (f32[768]{0:T(1024)}, f32[768]{0:T(1024)}, f32[768]{0:T(1024)}, f32[768]{0:T(1024)}) all-reduce(f32[768]{0:T(1024)} %get-tuple-element.14, f32[768]{0:T(1024)} %get-tuple-element.19, f32[768]{0:T(1024)S(1)} %copy-done.55, f32[768]{0:T(1024)} %get-tuple-element.18), channel_id=2, replica_groups=mesh['dp'=4,'seq'=8] {'seq'}, use_global_device_ids=true, to_apply=%region_24.25.clone | all-reduce | flops 3072 | bytes 24576
  1392.3 6.8 all-reduce.6
  1403.6 19.7 %all-reduce.22.cloned.1.call-done = (f32[96,768]{1,0:T(8,128)}, f32[96,768]{1,0:T(8,128)}, f32[96,768]{1,0:T(8,128)}, f32[96,768]{1,0:T(8,128)}, f32[96,3072]{1,0:T(8,128)}, /*index=5*/f32[384,768]{1,0:T(8,128)}) async-done(((f32[96,768]{1,0:T(8,128)}, f32[96,768]{1,0:T(8,128)}, f32[96,768]{1,0:T(8,128)}, f32[96,768]{1,0:T(8,128)}, f32[96,3072]{1,0:T(8,128)}, /*index=5*/f32[384,768]{1,0:T(8,128)}), ...) | async-done | bytes 3538960 | tf_op jit(solution)/shard_map/psum | solution.py:201
  (227 shorter events, 112.7 us)
Async XLA Ops:
  7.2 15.9 %copy-start = (bf16[768,768]{1,0:T(8,128)(2,1)S(1)}, bf16[768,768]{1,0:T(8,128)(2,1)}, u32[]{:S(2)}) copy-start(bf16[768,768]{1,0:T(8,128)(2,1)} %param.22) | copy-start | bytes 3538948
  7.2 102.2 %all-reduce.14.cloned.1.call-start = ((), (), s32[]{:S(2)}) async-start(), calls=%async_computation.6 | async-start | bytes 3145728 | tf_op jit(solution)/shard_map/psum | solution.py:99
  17.4 356.5 %all-reduce.20.cloned.1.call-start = ((), (), s32[]{:S(2)}) async-start(), calls=%async_computation.15 | async-start | bytes 12779520 | tf_op jit(solution)/shard_map/psum | solution.py:113
  23.0 86.4 %copy-start.12 = (bf16[4,128,12,64]{1,0,3,2:T(4,128)(2,1)}, bf16[4,128,12,64]{1,0,3,2:T(4,128)(2,1)S(1)}, u32[]{:S(2)}) copy-start(bf16[4,128,12,64]{1,0,3,2:T(4,128)(2,1)S(1)} %reshape.225) | copy-start | bytes 2359300
  69.6 43.7 %copy-start.38 = (f32[4,12,100]{2,1,0:T(8,128)}, f32[4,12,100]{2,1,0:T(8,128)S(1)}, u32[]{:S(2)}) copy-start(f32[4,12,100]{2,1,0:T(8,128)S(1)} %psum.113) | copy-start | bytes 57604
  151.3 9.6 copy-start.11
  160.9 459.5 %all-reduce.16.cloned.1.call-start = ((), (), s32[]{:S(2)}) async-start(), calls=%async_computation.7 | async-start | bytes 12582912 | tf_op jit(solution)/shard_map/psum | solution.py:151
  374.9 8.5 slice-start.2
  383.0 13.9 copy-start.8
  383.1 13.8 copy-start.46
  384.5 12.4 copy-start.49
  410.0 314.5 %all-reduce.18.cloned.1.call-start = ((), (), s32[]{:S(2)}) async-start(), calls=%async_computation.8 | async-start | bytes 3145728 | tf_op jit(solution)/shard_map/psum | solution.py:173
  620.4 7.0 copy-start.7
  620.4 7.0 copy-start.21
  620.4 7.0 copy-start.23
  620.4 7.0 copy-start.51
  636.4 160.2 %reduce-scatter.13.cloned.1.call-start = ((), (), s32[]{:S(2)}) async-start(), calls=%async_computation.12 | async-start | bytes 2654208 | tf_op jit(solution)/shard_map/reduce_scatter | solution.py:195
  639.9 228.6 %reduce-scatter.9.cloned.1.call-start = ((), (), s32[]{:S(2)}) async-start(), calls=%async_computation.10 | async-start | bytes 2654208 | tf_op jit(solution)/shard_map/reduce_scatter | solution.py:193
  647.7 292.8 %reduce-scatter.11.cloned.1.call-start = ((), (), s32[]{:S(2)}) async-start(), calls=%async_computation.11 | async-start | bytes 2654208 | tf_op jit(solution)/shard_map/reduce_scatter | solution.py:194
  656.0 356.5 %reduce-scatter.7.cloned.1.call-start = ((), (), s32[]{:S(2)}) async-start(), calls=%async_computation.9 | async-start | bytes 2654208 | tf_op jit(solution)/shard_map/reduce_scatter | solution.py:192
  731.4 447.5 %reduce-scatter.15.cloned.1.call-start = ((), (), s32[]{:S(2)}) async-start(), calls=%async_computation.13 | async-start | bytes 10616832 | tf_op jit(solution)/shard_map/reduce_scatter | solution.py:198
  741.0 604.2 %reduce-scatter.17.cloned.1.call-start = ((), (), s32[]{:S(2)}) async-start(), calls=%async_computation.14 | async-start | bytes 10616832 | tf_op jit(solution)/shard_map/reduce_scatter | solution.py:199
  750.9 672.4 %all-reduce.22.cloned.1.call-start = ((), (), s32[]{:S(2)}) async-start(), calls=%async_computation.16 | async-start | bytes 7077888 | tf_op jit(solution)/shard_map/psum | solution.py:201
  1423.3 5.9 copy-start.25
  (52 other events, 115.2 us)
Sparse Core Ops, SparseCore 0:
  17.5 91.8 all-reduce.13
  161.1 212.8 all-reduce.19
  410.1 210.2 all-reduce.15
  636.5 87.9 all-reduce.17
  728.2 68.3 reduce-scatter.12
  800.3 68.0 reduce-scatter.8
  872.3 68.0 reduce-scatter.10
  944.3 68.0 reduce-scatter.6
  1016.5 162.3 reduce-scatter.14
  1182.8 162.3 reduce-scatter.16
  1348.2 75.0 all-reduce.21
where the time goes:
time: 1450 us; the launch traced here: 1440 us
  waiting for transfers between devices  1120 us (77%)
  blocking collectives  118 us (8%)
  matrix products  113 us (8%)
  local copies, waits for them, and re-layouts  36.4 us (3%)
  other arithmetic  28.6 us (2%)
  between operations  15.8 us (1%)
    psum x1, waiting for transfers between devices, local(): grad_result = lax.psum(part_grad_result, 'seq')  210 us
    psum x1, waiting for transfers between devices, local(): summed, summed_denom = lax.psum((part_result, part_denom), 'seq')  204 us
    reduce_scatter x1, waiting for transfers between devices, local(): lax.psum_scatter(grad_w_up, 'seq', scatter_dimension=0, tiled=True)  166 us
    reduce_scatter x1, waiting for transfers between devices, local(): lax.psum_scatter(grad_w_down, 'seq', scatter_dimension=0, tiled=True)  166 us
    reduce_scatter x1, waiting for transfers between devices, local(): lax.psum_scatter(grad_w_query, 'seq', scatter_dimension=0, tiled=True)  72 us
    reduce_scatter x1, waiting for transfers between devices, local(): lax.psum_scatter(grad_w_value, 'seq', scatter_dimension=0, tiled=True)  72 us
    reduce_scatter x1, waiting for transfers between devices, local(): lax.psum_scatter(grad_w_key, 'seq', scatter_dimension=0, tiled=True)  71.9 us
    psum x1, waiting for transfers between devices, local(): grad_cent = lax.psum(part_grad_cent, 'seq')  68.5 us
  transfers between devices with their start and end apart: 11, of which 11 were waited for; matrix products, arithmetic and copies ran while one was open for 6% of the time, Pallas kernels for 0%

commit v1 on v0

v1 whole, which is shorter than its diff:
```python
import functools

import jax
import jax.numpy as jnp
from jax import lax
from jax.experimental import pallas as pl
from jax.experimental.pallas import tpu as pltpu
from jax.sharding import PartitionSpec as P

CLUSTERS = 100
PAD = 128
EPSILON = 1e-05
GELU_A = 0.7978845608028654
GELU_B = 0.044715
MESH = pl.DeviceIdType.MESH
F32 = jnp.float32
BF16 = jnp.bfloat16
VMEM_LIMIT = 60 * 2**20


class Plan:
    def __init__(self, mesh_shape, inputs, clusters, lengths, w_up):
        self.seq, self.dp = mesh_shape["seq"], mesh_shape["dp"]
        self.rows, self.part, self.width = inputs.shape
        self.heads, self.docs, self.hidden = clusters.shape[2], lengths.shape[1], w_up.shape[1]
        self.head = self.width // self.heads
        self.tokens = self.rows * self.part
        self.mates = self.seq // self.rows
        self.sent_docs = 1 if self.mates == 2 else self.docs
        self.block = self.width // self.seq
        self.fast = (
            self.dp == 4 and self.seq == 8 and self.block % 16 == 0 and self.hidden == 4 * self.width
        )

    def place(self, j):
        r, h = j // self.mates, j % self.mates
        if self.mates == 2:
            h = lax.rem(h + r, 2)
        return r, h

    def owner(self, r, h):
        if self.mates == 2:
            h = lax.rem(h + r, 2)
        return r * self.mates + h


def nn(a, b):
    return lax.dot_general(a, b, (((1,), (0,)), ((), ())), preferred_element_type=F32)


def nt(a, b):
    return lax.dot_general(a, b, (((1,), (1,)), ((), ())), preferred_element_type=F32)


def tn(a, b):
    return lax.dot_general(a, b, (((0,), (0,)), ((), ())), preferred_element_type=F32)


def remote(src, dst, send, recv, to):
    return pltpu.make_async_remote_copy(
        src_ref=src, dst_ref=dst, send_sem=send, recv_sem=recv, device_id=to, device_id_type=MESH
    )


def one_hot(row):
    ids = lax.broadcasted_iota(jnp.int32, (PAD, row.shape[1]), 0)
    return jnp.where(ids == row, 1.0, 0.0).astype(BF16)


def doc_masks(z, r, h, len_ref):
    pos = h * z.tokens + lax.broadcasted_iota(jnp.int32, (1, z.tokens), 1)
    seg = jnp.zeros((1, z.tokens), jnp.int32)
    end, ends = jnp.int32(0), []
    for s in range(z.docs):
        end = end + len_ref[r, s]
        ends.append(end)
        seg = seg + (pos >= end).astype(jnp.int32)
    last = sum((z.tokens - 1 >= e).astype(jnp.int32) for e in ends)
    first = sum((z.tokens >= e).astype(jnp.int32) for e in ends)
    spans = last == first
    mine = jnp.where(h == 0, last, first)
    return seg, spans, mine


def stacked_masks(z, seg):
    ids = lax.broadcasted_iota(jnp.int32, (z.docs * z.head, z.tokens), 0)
    body = jnp.where(ids // z.head == seg, 1.0, 0.0).astype(BF16)
    low = lax.broadcasted_iota(jnp.int32, (16, z.tokens), 0)
    tail = jnp.where((low % z.docs == seg) & (low < 2 * z.docs), 1.0, 0.0).astype(BF16)
    return body, tail


def pick_doc(z, blocks, mine):
    out = blocks[0]
    for s in range(1, z.docs):
        out = jnp.where(mine == s, blocks[s], out)
    return out


def mate_id(z, r, h, step):
    return {"seq": z.owner(r, lax.rem(h + step, z.mates))}


def greet_row(z, j):
    barrier = pltpu.get_barrier_semaphore()
    for d in range(1, z.seq):
        pl.semaphore_signal(
            barrier, 1, device_id={"seq": lax.rem(j + d, z.seq)}, device_id_type=MESH
        )
    return barrier


def scatter_rows(z, j, r, h, src, dst, send, recv, wait=False):
    slot = lax.rem(j, z.rows)
    for row in range(z.rows):
        to = z.owner(row, j // z.rows)

        @pl.when(to != j)
        def _():
            copy = remote(src.at[row], dst.at[slot], send.at[row], recv.at[slot], {"seq": to})
            if wait:
                copy.wait_send()
            else:
                copy.start()

        if not wait:

            @pl.when(to == j)
            def _():
                pltpu.make_async_copy(src.at[row], dst.at[slot], recv.at[slot]).start()


def landed(z, j, h, src, dst, send, recv, slot):
    source = h * z.rows + slot

    @pl.when(source == j)
    def _():
        pltpu.make_async_copy(src.at[0], dst.at[slot], recv.at[slot]).wait()

    @pl.when(source != j)
    def _():
        remote(
            src.at[0], dst.at[slot], send.at[0], recv.at[slot], {"seq": lax.rem(j + 1, z.seq)}
        ).wait_recv()


def norm_parts(values):
    average = jnp.mean(values, axis=-1, keepdims=True)
    centered = values - average
    inverse = lax.rsqrt(jnp.mean(centered * centered, axis=-1, keepdims=True) + EPSILON)
    return centered * inverse, inverse


def forward_kernel(
    z,
    x_ref, c_ref, clu_ref, len_ref, gain_ref, bias_ref, wq_ref, wk_ref, wv_ref,
    xrow, crow, n_t, k_t, v_t, att_t, wts, cent_t, cnts, res_t, rfac, clus,
    clu_in, q_t, body, sums, sums_in, u_s, big, big_in, small, small_in,
    x_send, x_recv, c_send, c_recv, i_send, i_recv, a_send, a_recv, b_send, b_recv, s_send, s_recv,
):
    j = lax.axis_index("seq")
    r, h = z.place(j)
    barrier = greet_row(z, j)
    seg, spans, mine = doc_masks(z, r, h, len_ref)
    body_value, tail = stacked_masks(z, seg)
    body[...] = body_value
    pl.semaphore_wait(barrier, z.seq - 1)
    scatter_rows(z, j, r, h, clu_ref, clu_in, i_send, i_recv)
    scatter_rows(z, j, r, h, x_ref, xrow, x_send, x_recv)

    def project(slot, carry):
        landed(z, j, h, x_ref, xrow, x_send, x_recv, slot)
        unit, _ = norm_parts(xrow[slot].astype(F32))
        normed = (unit * gain_ref[...] + bias_ref[...]).astype(BF16)
        where = pl.ds(pl.multiple_of(slot * z.part, z.part), z.part)
        n_t[:, where] = normed.T
        for w_ref, out in ((wq_ref, q_t), (wk_ref, k_t), (wv_ref, v_t)):
            out[:, where] = nn(normed, w_ref[...]).astype(BF16).T
        return carry

    lax.fori_loop(0, z.rows, project, 0)
    for slot in range(z.rows):
        landed(z, j, h, clu_ref, clu_in, i_send, i_recv, slot)
        clus[:, slot * z.part : (slot + 1) * z.part] = clu_in[slot]
    scatter_rows(z, j, r, h, x_ref, xrow, x_send, x_recv, wait=True)
    scatter_rows(z, j, r, h, clu_ref, clu_in, i_send, i_recv, wait=True)
    scatter_rows(z, j, r, h, c_ref, crow, c_send, c_recv)

    ones = jnp.ones((16, z.tokens), BF16)

    def sum_copy(i, step):
        return remote(
            sums.at[i], sums_in.at[step - 1, i], a_send.at[step - 1, i], a_recv.at[step - 1, i],
            mate_id(z, r, h, step),
        )

    def result_copies(i, step):
        to = mate_id(z, r, h, step)
        return (
            remote(big.at[i], big_in.at[step - 1, i], b_send.at[step - 1, i], b_recv.at[step - 1, i], to),
            remote(small.at[i], small_in.at[step - 1, i], s_send.at[step - 1, i], s_recv.at[step - 1, i], to),
        )

    def head_rows(i):
        return pl.ds(pl.multiple_of(i * z.head, z.head), z.head)

    def cluster_sums(i, carry):
        member = one_hot(clus[pl.ds(i, 1), :])
        both = nt(jnp.concatenate([q_t[head_rows(i), :], ones], axis=0), member)
        sums[i] = both[: z.head + 8]
        for step in range(1, z.mates):
            sum_copy(i, step).start()
        return carry

    lax.fori_loop(0, z.heads, cluster_sums, 0)

    def attend(i, carry):
        total = sums[i]
        for step in range(1, z.mates):
            sum_copy(i, step).wait()
            total = total + sums_in[step - 1, i]
        count = jnp.maximum(total[z.head :], 1.0)
        cent = (total[: z.head] / count[0:1]).astype(BF16)
        cent_t[i] = cent
        cnts[i] = count
        scores = tn(cent, k_t[head_rows(i), :]) * 0.125
        top = jnp.max(scores, axis=1, keepdims=True)
        weights = jnp.exp(scores - top).astype(BF16)
        wts[i] = weights
        value = v_t[head_rows(i), :]
        masked = jnp.concatenate([value] * z.docs, axis=0) * body[...]
        both = nt(jnp.concatenate([masked, tail], axis=0), weights)
        u_s[i] = both[: z.docs * z.head]
        top_row = jnp.broadcast_to(top, (PAD, PAD)).T
        small[i] = jnp.concatenate([both[z.docs * z.head : z.docs * z.head + 4], top_row[:4]], axis=0)
        if z.mates == 2:
            parts = [both[s * z.head : (s + 1) * z.head] for s in range(z.docs)]
            big[i] = pick_doc(z, parts, mine).astype(BF16)
        else:
            big[i] = both[: z.docs * z.head].astype(BF16)
        for step in range(1, z.mates):
            for copy in result_copies(i, step):
                copy.start()
        return carry

    lax.fori_loop(0, z.heads, attend, 0)
    empty = [jnp.where(jnp.sum((seg == s).astype(F32)) > 0.5, 0.0, 1.0) for s in range(z.docs)]

    def finish(i, carry):
        own = small[i]
        top, denoms = own[4:5], own[:4]
        highest = top
        for step in range(1, z.mates):
            for copy in result_copies(i, step):
                copy.wait()
            highest = jnp.maximum(highest, small_in[step - 1, i][4:5])
        scale = jnp.exp(top - highest)
        member = one_hot(clus[pl.ds(i, 1), :])
        scaled, factors = [], []
        for s in range(z.docs):
            part = u_s[i, s * z.head : (s + 1) * z.head]
            denom = denoms[s : s + 1]
            joined, joined_denom = part * scale, denom * scale
            for step in range(1, z.mates):
                other = small_in[step - 1, i]
                other_scale = jnp.exp(other[4:5] - highest)
                lo = 0 if z.mates == 2 else s * z.head
                joined = joined + big_in[step - 1, i][lo : lo + z.head].astype(F32) * other_scale
                joined_denom = joined_denom + other[s : s + 1] * other_scale
            if z.mates == 2:
                here = jnp.logical_and(spans, mine == s)
            else:
                here = True
            joined = jnp.where(here, joined, part)
            joined_denom = jnp.where(here, joined_denom, denom)
            factor = jnp.where(here, scale, jnp.ones_like(scale))
            joined_denom = joined_denom + jnp.where(joined_denom > 0.0, 0.0, empty[s])
            inverse = 1.0 / joined_denom
            scaled.append((joined * inverse).astype(BF16))
            factors.append(inverse * factor)
        result = jnp.concatenate(scaled, axis=0)
        res_t[i] = result
        rfac[i] = jnp.concatenate(factors + [jnp.zeros((8 - z.docs, PAD), F32)], axis=0)
        picked = nn(result, member)
        out = picked[: z.head]
        for s in range(1, z.docs):
            out = jnp.where(seg == s, picked[s * z.head : (s + 1) * z.head], out)
        att_t[head_rows(i), :] = out.astype(BF16)
        return carry

    lax.fori_loop(0, z.heads, finish, 0)
    for slot in range(z.rows):
        landed(z, j, h, c_ref, crow, c_send, c_recv, slot)
    scatter_rows(z, j, r, h, c_ref, crow, c_send, c_recv, wait=True)


def middle_kernel(
    z,
    xrow, crow, att_t, wo_ref, gain_ref, bias_ref, up_ref, down_ref,
    out_ref, gm_ref, ga_t, d_out, d_up, d_down, vec_ref,
    low, low_t, g_low, act, gp, acc, acc_n,
):
    width, part = z.width, z.part
    total = z.tokens

    def first(t, carry):
        rows = pl.ds(pl.multiple_of(t * part, part), part)
        middle = xrow[t].astype(F32) + tn(att_t[:, rows], wo_ref[...])
        acc[rows, :] = middle
        gm_ref[rows, :] = middle
        unit, _ = norm_parts(middle)
        normed = (unit * gain_ref[...] + bias_ref[...]).astype(BF16)
        low[rows, :] = normed
        low_t[:, rows] = normed.T
        g_low[rows, :] = crow[t]
        return carry

    lax.fori_loop(0, z.rows, first, 0)
    acc_n[...] = jnp.zeros_like(acc_n)

    def chunk(f, carry):
        cols = pl.ds(pl.multiple_of(f * width, width), width)
        half = total // 2
        for t in range(2):
            rows = slice(t * half, (t + 1) * half)
            u = nn(low[rows, :], up_ref[:, cols])
            tanh = jnp.tanh(GELU_A * (u + GELU_B * (u * u * u)))
            cdf = 0.5 * (1.0 + tanh)
            act[rows, :] = (u * cdf).astype(BF16)
            slope = cdf + (0.5 * GELU_A) * u * (1.0 - tanh * tanh) * (1.0 + (3.0 * GELU_B) * (u * u))
            grad = nt(g_low[rows, :], down_ref[cols, :])
            gp[rows, :] = (grad * slope).astype(BF16)
            acc[rows, :] += nn(act[rows, :], down_ref[cols, :])
            acc_n[rows, :] += nt(gp[rows, :], up_ref[:, cols])
        d_up[f] = nn(low_t[...], gp[...]).astype(BF16).reshape(d_up.shape[1:])
        piece = tn(act[...], g_low[...]).astype(BF16)
        if z.fast:
            rows_of = z.hidden // (z.seq * z.dp)
            per = width // (rows_of * z.dp)
            for jj in range(per):
                for p in range(z.dp):
                    at = (jj * z.dp + p) * rows_of
                    d_down[p, f * per + jj] = piece[at : at + rows_of]
        else:
            d_down[cols, :] = piece
        return carry

    lax.fori_loop(0, z.hidden // width, chunk, 0)

    def last(t, carry):
        rows = pl.ds(pl.multiple_of(t * part, part), part)
        out_ref[t] = acc[rows, :].astype(BF16)
        unit, inverse = norm_parts(gm_ref[rows, :])
        grad = acc_n[rows, :]
        scaled = grad * gain_ref[...]
        inner = (
            scaled
            - jnp.mean(scaled, axis=-1, keepdims=True)
            - unit * jnp.mean(scaled * unit, axis=-1, keepdims=True)
        )
        grad_middle = g_low[rows, :].astype(F32) + inner * inverse
        gm_ref[rows, :] = grad_middle
        low[rows, :] = grad_middle.astype(BF16)
        return (
            carry[0] + jnp.sum(grad * unit, axis=0, keepdims=True),
            carry[1] + jnp.sum(grad, axis=0, keepdims=True),
        )

    zero = jnp.zeros((1, width), F32)
    grad_gain, grad_bias = lax.fori_loop(0, z.rows, last, (zero, zero))
    vec_ref[...] = jnp.concatenate([grad_gain, grad_bias], axis=0)
    d_out[...] = nn(att_t[...], low[...]).astype(BF16).reshape(d_out.shape)
    ga_t[...] = nt(wo_ref[...], low[...]).astype(BF16)


def backward_kernel(
    z,
    len_ref, xrow, gm_ref, n_t, k_t, v_t, wts, cent_t, cnts, res_t, rfac, clus, ga_t,
    gain_ref, wq_ref, wk_ref, wv_ref, d_out, d_up, d_down, vec_in, out_rows,
    out_ref, gx_ref, w_qkvo, w_up_ref, w_down_ref, vec_ref,
    body, g_s, g_send, g_recv, c_s, c_recv, gq_t, gk_t, gv_t, acc, x_part,
    dq, crecv, yrecv, xrecv, zrecv, gat, vec_buf, vec_got,
    o_send, o_recv, x_send, x_recv, ga_ss, ga_rs, gc_ss, gc_rs,
    core_s, core_r, y_s, y_r, x_s, x_r, z_s, z_r, dp_s, dp_r, v_s, v_r,
):
    j = lax.axis_index("seq")
    me = lax.axis_index("dp")
    r, h = z.place(j)
    barrier = greet_row(z, j)
    greeted = z.seq - 1
    if z.fast:
        for d in range(1, z.dp):
            pl.semaphore_signal(
                barrier, 1, device_id={"dp": lax.rem(me + d, z.dp)}, device_id_type=MESH
            )
        greeted += z.dp - 1
    seg, spans, mine = doc_masks(z, r, h, len_ref)
    body_value, tail = stacked_masks(z, seg)
    body[...] = body_value
    pl.semaphore_wait(barrier, greeted)

    core, y = lax.rem(me, 2), me // 2
    xx, zz = lax.rem(j, 2), j // 2
    sibling, across = me + 1 - 2 * core, me + 2 - 4 * y
    lanes_of_z = z.seq // 2
    grads = (d_down, d_up, dq)

    def core_copy(g, t):
        yy = (1 - y) if t == 0 else y
        return remote(
            grads[g].at[yy * 2 + 1 - core], crecv.at[g, t], core_s.at[g, t], core_r.at[g, t], {"dp": sibling}
        )

    def y_copy(g, b):
        return remote(
            crecv.at[g, 0, b], yrecv.at[g, b], y_s.at[g, b], y_r.at[g, b], {"dp": across}
        )

    def x_copy(g, k):
        return remote(
            crecv.at[g, 1, 2 * k + 1 - xx], xrecv.at[g, k], x_s.at[g, k], x_r.at[g, k],
            {"seq": j + 1 - 2 * xx},
        )

    def z_copy(g, k):
        to = lax.rem(zz + k, lanes_of_z) * 2 + xx
        return remote(
            crecv.at[g, 1, to], zrecv.at[g, k - 1], z_s.at[g, k - 1], z_r.at[g, k - 1], {"seq": to}
        )

    def dp_copy(g, k):
        return remote(
            gat.at[g, me], gat.at[g, me], dp_s.at[g, k - 1], dp_r.at[g, k - 1],
            {"dp": lax.rem(me + k, z.dp)},
        )

    def dp_wait(g, k):
        source = lax.rem(me + z.dp - k, z.dp)
        remote(
            gat.at[g, source], gat.at[g, source], dp_s.at[g, k - 1], dp_r.at[g, k - 1],
            {"dp": lax.rem(me + k, z.dp)},
        ).wait_recv()

    def add(ref, value):
        ref[...] = (ref[...].astype(F32) + value.astype(F32)).astype(BF16)

    def core_start(g):
        for t in range(2):
            core_copy(g, t).start()

    def block_order(i):
        return lax.rem(i, lanes_of_z) * 2 + jnp.where(i < lanes_of_z, 1 - xx, xx)

    def core_finish(g):
        core_copy(g, 0).wait_recv()

        def forward(i, carry):
            b = block_order(i)
            add(crecv.at[g, 0, b], grads[g][across, b])
            y_copy(g, b).start()
            return carry

        lax.fori_loop(0, z.seq, forward, 0)
        core_copy(g, 1).wait_recv()

        def keep(b, carry):
            add(crecv.at[g, 1, b], grads[g][me, b])
            return carry

        lax.fori_loop(0, z.seq, keep, 0)

    def y_finish(g):
        def away(k, carry):
            b = 2 * k + 1 - xx
            y_copy(g, b).wait_recv()
            add(crecv.at[g, 1, b], yrecv[g, b])
            x_copy(g, k).start()
            return carry

        def keep(k, carry):
            b = 2 * k + xx
            y_copy(g, b).wait_recv()
            add(crecv.at[g, 1, b], yrecv[g, b])
            return carry

        lax.fori_loop(0, lanes_of_z, away, 0)
        lax.fori_loop(0, lanes_of_z, keep, 0)

    def x_finish(g):
        for k in list(range(1, lanes_of_z)) + [0]:
            to = lax.rem(zz + k, lanes_of_z)
            x_copy(g, to).wait_recv()
            add(crecv.at[g, 1, 2 * to + xx], xrecv[g, to])
            if k:
                z_copy(g, k).start()

    def z_finish(g):
        total = crecv[g, 1, j].astype(F32)
        for k in range(1, lanes_of_z):
            z_copy(g, k).wait_recv()
            total = total + zrecv[g, k - 1].astype(F32)
        gat[g, me] = total.astype(BF16)
        for k in range(1, z.dp):
            dp_copy(g, k).start()

    def dp_finish(g):
        for k in range(1, z.dp):
            dp_wait(g, k)
        for p in range(z.dp):
            block = gat[g, p].astype(F32)
            if g == 0:
                w_down_ref[p * z.block : (p + 1) * z.block, :] = block
            elif g == 1:
                w_up_ref[:, p * z.width : (p + 1) * z.width] = block
            else:
                w_qkvo[p] = block

    def sent(g):
        for t in range(2):
            core_copy(g, t).wait_send()

        def y_sent(b, carry):
            y_copy(g, b).wait_send()
            return carry

        lax.fori_loop(0, z.seq, y_sent, 0)

        def x_sent(k, carry):
            x_copy(g, k).wait_send()
            return carry

        lax.fori_loop(0, lanes_of_z, x_sent, 0)
        for k in range(1, lanes_of_z):
            z_copy(g, k).wait_send()
        for k in range(1, z.dp):
            dp_copy(g, k).wait_send()

    if z.fast:
        core_start(0)
        core_start(1)

    def back(slot):
        return h * z.rows + slot

    def rows_back(src, dst, send, recv, wait=False):
        for slot in range(z.rows):
            to = back(slot)

            @pl.when(to != j)
            def _():
                copy = remote(src.at[slot], dst.at[r], send.at[slot], recv.at[r], {"seq": to})
                if wait:
                    copy.wait_send()
                else:
                    copy.start()

            if not wait:

                @pl.when(to == j)
                def _():
                    pltpu.make_async_copy(src.at[slot], dst.at[r], recv.at[r]).start()

    def rows_landed(src, dst, send, recv):
        for row in range(z.rows):
            source = z.owner(row, j // z.rows)

            @pl.when(source == j)
            def _():
                pltpu.make_async_copy(src.at[0], dst.at[row], recv.at[row]).wait()

            @pl.when(source != j)
            def _():
                remote(
                    src.at[0], dst.at[row], send.at[0], recv.at[row], {"seq": lax.rem(j + 1, z.seq)}
                ).wait_recv()

    rows_back(out_rows, out_ref, o_send, o_recv)

    def head_rows(i):
        return pl.ds(pl.multiple_of(i * z.head, z.head), z.head)

    def grad_copy(i, step):
        return remote(
            g_send.at[i], g_recv.at[step - 1, i], ga_ss.at[step - 1, i], ga_rs.at[step - 1, i],
            mate_id(z, r, h, step),
        )

    def cent_copy(i, step):
        return remote(
            c_s.at[i], c_recv.at[step - 1, i], gc_ss.at[step - 1, i], gc_rs.at[step - 1, i],
            mate_id(z, r, h, step),
        )

    def gather_grads(i, carry):
        member = one_hot(clus[pl.ds(i, 1), :])
        masked = jnp.concatenate([ga_t[head_rows(i), :]] * z.docs, axis=0) * body[...]
        both = nt(masked, member)
        g_s[i] = both
        if z.mates == 2:
            parts = [both[s * z.head : (s + 1) * z.head] for s in range(z.docs)]
            g_send[i] = pick_doc(z, parts, mine).astype(BF16)
        else:
            g_send[i] = both.astype(BF16)
        for step in range(1, z.mates):
            grad_copy(i, step).start()
        return carry

    lax.fori_loop(0, z.heads, gather_grads, 0)
    if z.fast:
        core_finish(0)
        core_finish(1)

    def attend_back(i, carry):
        for step in range(1, z.mates):
            grad_copy(i, step).wait()
        result, factor = res_t[i], rfac[i]
        lows, deltas = [], []
        for s in range(z.docs):
            grad = g_s[i, s * z.head : (s + 1) * z.head]
            joined = grad
            for step in range(1, z.mates):
                lo = 0 if z.mates == 2 else s * z.head
                joined = joined + g_recv[step - 1, i][lo : lo + z.head].astype(F32)
            if z.mates == 2:
                joined = jnp.where(jnp.logical_and(spans, mine == s), joined, grad)
            scaled = joined * factor[s : s + 1]
            lows.append(scaled.astype(BF16))
            part = result[s * z.head : (s + 1) * z.head].astype(F32)
            deltas.append(-jnp.sum(scaled * part, axis=0, keepdims=True))
        delta = jnp.concatenate(deltas, axis=0)
        high = delta.astype(BF16)
        rest = (delta - high.astype(F32)).astype(BF16)
        small = jnp.concatenate(
            [high.astype(F32), rest.astype(F32), jnp.zeros((16 - 2 * z.docs, PAD), F32)], axis=0
        ).astype(BF16)
        low = jnp.concatenate(lows, axis=0)
        value = v_t[head_rows(i), :]
        masked = jnp.concatenate([value] * z.docs, axis=0) * body[...]
        diff = tn(
            jnp.concatenate([low, small], axis=0), jnp.concatenate([masked, tail], axis=0)
        )
        weights = wts[i]
        raw = (0.125 * (weights.astype(F32) * diff)).astype(BF16)
        gk_t[head_rows(i), :] = nn(cent_t[i], raw).astype(BF16)
        spread = nn(low, weights)
        out = spread[: z.head]
        for s in range(1, z.docs):
            out = jnp.where(seg == s, spread[s * z.head : (s + 1) * z.head], out)
        gv_t[head_rows(i), :] = out.astype(BF16)
        c_s[i] = nt(k_t[head_rows(i), :], raw)
        for step in range(1, z.mates):
            cent_copy(i, step).start()
        return carry

    lax.fori_loop(0, z.heads, attend_back, 0)

    def query_back(i, carry):
        total = c_s[i]
        for step in range(1, z.mates):
            cent_copy(i, step).wait()
            total = total + c_recv[step - 1, i]
        member = one_hot(clus[pl.ds(i, 1), :])
        gq_t[head_rows(i), :] = nn((total / cnts[i, 0:1]).astype(BF16), member).astype(BF16)
        return carry

    lax.fori_loop(0, z.heads, query_back, 0)

    for p, g_ref in enumerate((gq_t, gk_t, gv_t)):
        dq[p] = nt(n_t[...], g_ref[...]).astype(BF16).reshape(dq.shape[1:])
    dq[3] = d_out[...]
    if z.fast:
        core_start(2)
    total = nn(wq_ref[...], gq_t[...]) + nn(wk_ref[...], gk_t[...]) + nn(wv_ref[...], gv_t[...])
    acc[...] = total.T

    def last(t, carry):
        rows = pl.ds(pl.multiple_of(t * z.part, z.part), z.part)
        unit, inverse = norm_parts(xrow[t].astype(F32))
        grad = acc[rows, :]
        scaled = grad * gain_ref[...]
        inner = (
            scaled
            - jnp.mean(scaled, axis=-1, keepdims=True)
            - unit * jnp.mean(scaled * unit, axis=-1, keepdims=True)
        )
        x_part[t] = (gm_ref[rows, :] + inner * inverse).astype(BF16)
        return (
            carry[0] + jnp.sum(grad * unit, axis=0, keepdims=True),
            carry[1] + jnp.sum(grad, axis=0, keepdims=True),
        )

    zero = jnp.zeros((1, z.width), F32)
    grad_gain, grad_bias = lax.fori_loop(0, z.rows, last, (zero, zero))
    vectors = jnp.concatenate([grad_gain, grad_bias, vec_in[...], jnp.zeros((4, z.width), F32)], axis=0)
    rows_back(x_part, gx_ref, x_send, x_recv)

    if z.fast:
        core_finish(2)
        y_finish(0)
        y_finish(1)
        x_finish(0)
        x_finish(1)
        y_finish(2)
        z_finish(0)
        z_finish(1)
        x_finish(2)
        z_finish(2)

        def vec_copy(t, to):
            return remote(vec_buf.at[min(t, 2)], vec_got.at[t], v_s.at[t], v_r.at[t], to)

        vec_buf[0] = vectors
        copy = vec_copy(0, {"dp": sibling})
        copy.start()
        copy.wait()
        vec_buf[1] = vec_buf[0] + vec_got[0]
        copy = vec_copy(1, {"dp": across})
        copy.start()
        copy.wait()
        vec_buf[2] = vec_buf[1] + vec_got[1]
        copies = [vec_copy(1 + d, {"seq": lax.rem(j + d, z.seq)}) for d in range(1, z.seq)]
        for copy in copies:
            copy.start()
        total = vec_buf[2]
        for d, copy in enumerate(copies):
            copy.wait()
            total = total + vec_got[2 + d]
        vec_ref[...] = total
        for g in range(3):
            dp_finish(g)
        for g in range(3):
            sent(g)
    else:
        vec_ref[...] = vectors
        for p in range(4):
            w_qkvo[p] = dq[p].astype(F32)

    rows_landed(out_rows, out_ref, o_send, o_recv)
    rows_landed(x_part, gx_ref, x_send, x_recv)
    rows_back(out_rows, out_ref, o_send, o_recv, wait=True)
    rows_back(x_part, gx_ref, x_send, x_recv, wait=True)


def local(
    mesh_shape,
    inputs, cotangent, lengths, clusters, gain_attn, bias_attn, w_query, w_key, w_value, w_out,
    gain_ffn, bias_ffn, w_up, w_down,
):
    z = Plan(mesh_shape, inputs, clusters, lengths, w_up)
    width, tokens, heads, mates, docs = z.width, z.tokens, z.heads, z.mates, z.docs
    any_space = pl.BlockSpec(memory_space=pl.ANY)
    vmem = pl.BlockSpec(memory_space=pltpu.VMEM)
    smem = pl.BlockSpec(memory_space=pltpu.SMEM)
    dma = pltpu.SemaphoreType.DMA
    shape = jax.ShapeDtypeStruct
    high_heads = -(-heads // 8) * 8
    turned = jnp.pad(jnp.transpose(clusters, (0, 2, 1)), ((0, 0), (0, high_heads - heads), (0, 0)))
    flat = lambda v: v.reshape(1, -1)
    row_like = shape((z.rows, z.part, width), BF16)
    long = shape((width, tokens), BF16)
    others = mates - 1
    xrow, crow, n_t, k_t, v_t, att_t, wts, cent_t, cnts, res_t, rfac, clus = pl.pallas_call(
        functools.partial(forward_kernel, z),
        out_shape=(
            row_like, row_like, long, long, long, long,
            shape((heads, PAD, tokens), BF16),
            shape((heads, z.head, PAD), BF16),
            shape((heads, 8, PAD), F32),
            shape((heads, docs * z.head, PAD), BF16),
            shape((heads, 8, PAD), F32),
            shape((high_heads, tokens), jnp.int32),
        ),
        in_specs=[any_space, any_space, any_space, smem] + [vmem] * 5,
        out_specs=[vmem] * 12,
        scratch_shapes=[
            pltpu.VMEM((z.rows, high_heads, z.part), jnp.int32),
            pltpu.VMEM((width, tokens), BF16),
            pltpu.VMEM((docs * z.head, tokens), BF16),
            pltpu.VMEM((heads, z.head + 8, PAD), F32),
            pltpu.VMEM((others, heads, z.head + 8, PAD), F32),
            pltpu.VMEM((heads, docs * z.head, PAD), F32),
            pltpu.VMEM((heads, z.sent_docs * z.head, PAD), BF16),
            pltpu.VMEM((others, heads, z.sent_docs * z.head, PAD), BF16),
            pltpu.VMEM((heads, 8, PAD), F32),
            pltpu.VMEM((others, heads, 8, PAD), F32),
        ]
        + [dma((z.rows,))] * 6
        + [dma((others, heads))] * 6,
        compiler_params=pltpu.CompilerParams(
            collective_id=0, has_side_effects=True, vmem_limit_bytes=VMEM_LIMIT
        ),
    )(
        inputs, cotangent, turned, lengths, flat(gain_attn), flat(bias_attn), w_query, w_key, w_value
    )

    if z.fast:
        square = shape((z.seq, z.block, width), BF16)
        up_shape = shape((4, z.seq, z.block, width), BF16)
        down_shape = shape((z.dp, z.seq, z.hidden // (z.seq * z.dp), width), BF16)
    else:
        square = shape((width, width), BF16)
        up_shape = shape((z.hidden // width, width, width), BF16)
        down_shape = shape((z.hidden, width), BF16)
    out_rows, gm, ga_t, d_out, d_up, d_down, vec_ffn = pl.pallas_call(
        functools.partial(middle_kernel, z),
        out_shape=(
            row_like, shape((tokens, width), F32), long, square, up_shape, down_shape,
            shape((2, width), F32),
        ),
        in_specs=[vmem] * 8,
        out_specs=[vmem] * 7,
        scratch_shapes=[
            pltpu.VMEM((tokens, width), BF16),
            pltpu.VMEM((width, tokens), BF16),
            pltpu.VMEM((tokens, width), BF16),
            pltpu.VMEM((tokens, width), BF16),
            pltpu.VMEM((tokens, width), BF16),
            pltpu.VMEM((tokens, width), F32),
            pltpu.VMEM((tokens, width), F32),
        ],
        compiler_params=pltpu.CompilerParams(vmem_limit_bytes=VMEM_LIMIT),
    )(xrow, crow, att_t, w_out, flat(gain_ffn), flat(bias_ffn), w_up, w_down)

    if z.fast:
        outs = (
            shape((4, z.block, width), F32),
            shape((z.block, z.hidden), F32),
            shape((z.hidden // z.seq, width), F32),
        )
        rs = [
            pltpu.VMEM((4, z.seq, z.block, width), BF16),
            pltpu.VMEM((3, 2, z.seq, z.block, width), BF16),
            pltpu.VMEM((3, z.seq, z.block, width), BF16),
            pltpu.VMEM((3, z.seq // 2, z.block, width), BF16),
            pltpu.VMEM((3, z.seq // 2 - 1, z.block, width), BF16),
            pltpu.VMEM((3, z.dp, z.block, width), BF16),
        ]
        wide = vmem
    else:
        outs = (shape((4, width, width), F32), shape((8, PAD), F32), shape((8, PAD), F32))
        rs = [pltpu.VMEM((4, width, width), BF16)] + [pltpu.VMEM((8, PAD), BF16)] * 5
        wide = any_space
    out_back, grad_back, g_qkvo, g_up, g_down, vectors = pl.pallas_call(
        functools.partial(backward_kernel, z),
        out_shape=(row_like, row_like) + outs + (shape((8, width), F32),),
        in_specs=[smem] + [vmem] * 17 + [wide, wide] + [vmem] * 2,
        out_specs=[vmem] * 6,
        scratch_shapes=[
            pltpu.VMEM((docs * z.head, tokens), BF16),
            pltpu.VMEM((heads, docs * z.head, PAD), F32),
            pltpu.VMEM((heads, z.sent_docs * z.head, PAD), BF16),
            pltpu.VMEM((others, heads, z.sent_docs * z.head, PAD), BF16),
            pltpu.VMEM((heads, z.head, PAD), F32),
            pltpu.VMEM((others, heads, z.head, PAD), F32),
            pltpu.VMEM((width, tokens), BF16),
            pltpu.VMEM((width, tokens), BF16),
            pltpu.VMEM((width, tokens), BF16),
            pltpu.VMEM((tokens, width), F32),
            pltpu.VMEM((z.rows, z.part, width), BF16),
        ]
        + rs
        + [pltpu.VMEM((3, 8, width), F32), pltpu.VMEM((z.seq + 1, 8, width), F32)]
        + [dma((z.rows,))] * 4
        + [dma((others, heads))] * 4
        + [dma((3, 2))] * 2
        + [dma((3, z.seq))] * 2
        + [dma((3, z.seq // 2))] * 4
        + [dma((3, z.dp))] * 2
        + [dma((z.seq + 1,))] * 2,
        compiler_params=pltpu.CompilerParams(
            collective_id=1, has_side_effects=True, vmem_limit_bytes=VMEM_LIMIT
        ),
    )(
        lengths, xrow, gm, n_t, k_t, v_t, wts, cent_t, cnts, res_t, rfac, clus, ga_t,
        flat(gain_attn), w_query, w_key, w_value, d_out, d_up, d_down, vec_ffn, out_rows,
    )

    if z.fast:
        own = lax.dynamic_slice_in_dim(vectors, lax.axis_index("seq") * z.block, z.block, 1)
    else:
        wide_up = jnp.transpose(d_up, (1, 0, 2)).reshape(width, z.hidden)

        def share(v, dim):
            v = lax.psum_scatter(v.astype(F32), "seq", scatter_dimension=dim, tiled=True)
            return lax.psum(v, "dp")

        g_qkvo, g_up, g_down, own = (
            share(g_qkvo, 1), share(wide_up, 0), share(d_down, 0), share(vectors, 1),
        )
    return (
        out_back.astype(F32), grad_back.astype(F32), own[0], own[1],
        g_qkvo[0], g_qkvo[1], g_qkvo[2], g_qkvo[3], own[2], own[3], g_up, g_down,
    )


def solution(mesh):
    spread = P("dp", "seq", None)
    return jax.shard_map(
        functools.partial(local, dict(mesh.shape)),
        mesh=mesh,
        in_specs=(spread, spread, P("dp", None), spread) + (P(),) * 10,
        out_specs=(spread, spread, P("seq"), P("seq")) + (P("seq", None),) * 4
        + (P("seq"), P("seq"), P("seq", None), P("seq", None)),
        check_vma=False,
    )
```

time: 1450 us -> 232 us (0.16)
  waiting for transfers between devices: 1120 us -> 0 us
  Pallas kernels: 0 us -> 217 us
  blocking collectives: 118 us -> 0 us
  matrix products: 113 us -> 0 us
  local copies, waits for them, and re-layouts: 36.4 us -> 10.6 us
  other arithmetic: 28.6 us -> 3.75 us
  between operations: 15.8 us -> 0.69 us
    reduce_scatter x6 -> x0, waiting for transfers between devices: 583 us -> none  [the longest x1 166 us: local(): lax.psum_scatter(grad_w_up, 'seq', scatter_dimension=0, tiled=True)]
    psum x5 -> x0, waiting for transfers between devices: 542 us -> none  [the longest x1 210 us: local(): grad_result = lax.psum(part_grad_result, 'seq')]
    pallas_call x0 -> x3, Pallas kernels: none -> 217 us  [the longest x1 129 us: local(): pl.pallas_call(functools.partial(backward_kernel, z), out_shape=(row_like...]
    dot_general x30 -> x0, matrix products: 113 us -> none  [the longest x6 28.9 us: inner_rows(): lax.dot_general(left, right, (((0,), (0,)), ((), ())), preferred_element_...]
    psum x2 -> x0, blocking collectives: 46.4 us -> none  [the longest x1 39.6 us: local(): sums, counts = lax.psum((part_sums, part_counts), 'seq')]
    unnamed x1 -> x0, blocking collectives: 35.7 us -> none
    pmax x1 -> x0, blocking collectives: 35.5 us -> none  [local(): row_max = lax.pmax(jnp.max(scores, axis=3), 'seq')]
    unnamed x142 -> x15, local copies, waits for them, and re-layouts: 24.9 us -> 3.99 us
  transfers between devices with their start and end apart: 11 -> 0, of which waited for: 11 -> 0; matrix products, arithmetic and copies ran while one was open for 6% -> 0% of each run, Pallas kernels for 0% -> 0%
where the time goes in v1:
time: 232 us
  Pallas kernels  217 us (94%)
  local copies, waits for them, and re-layouts  10.6 us (5%)
  other arithmetic  3.75 us (2%)
    pallas_call x1, Pallas kernels, local(): pl.pallas_call(functools.partial(backward_kernel, z), out_shape=(row_like...  129 us
    pallas_call x1, Pallas kernels, local(): pl.pallas_call(functools.partial(forward_kernel, z), out_shape=(row_like,...  56.6 us
    pallas_call x1, Pallas kernels, local(): pl.pallas_call(functools.partial(middle_kernel, z), out_shape=(row_like,...  31.3 us

profile of v1, /device:TPU:0, one launch (start us, length us, event | category | flops | bytes accessed | tf_op | source)
XLA Modules:
  0.0 231.6 jit_solution(2319062115669181895)
XLA Ops:
  0.6 1.3 reshape.37.gain_ref
  1.9 0.7 copy.28
  2.7 0.6 pad.4.clu_ref
  3.3 1.3 reshape.38.bias_ref
  4.5 0.0 copy-start.4
  4.5 56.6 %shard_map.229 = (bf16[4,128,768]{2,1,0:T(8,128)(2,1)}, bf16[4,128,768]{2,1,0:T(8,128)(2,1)}, bf16[768,512]{1,0:T(8,128)(2,1)}, bf16[768,512]{1,0:T(8,128)(2,1)}...) custom-call(bf16[4,128,768]{2,1,0:T(8,128)(2,1)} %x_ref.1, ...), custom_call_target="tpu_custom_call" | custom-call | tf_op jit(solution)/shard_map/pallas_call | solution.py:762
  61.2 0.0 copy-done.4
  61.2 0.6 reshape.39.gain_ref
  61.8 0.0 copy-done.5
  61.8 0.6 reshape.40.bias_ref
  62.4 31.3 %shard_map.230 = (bf16[4,128,768]{2,1,0:T(8,128)(2,1)}, f32[512,768]{1,0:T(8,128)}, bf16[768,512]{1,0:T(8,128)(2,1)}, bf16[8,96,768]{2,1,0:T(8,128)(2,1)}, bf16[...) custom-call(bf16[4,128,768]{2,1,0:T(8,128)(2,1)} %get-tuple-element.37.xrow, ...), custom_call_target="tpu_custom_call" | custom-call | tf_op jit(solution)/shard_map/pallas_call | solution.py:804
  93.7 128.6 %shard_map.231 = (bf16[4,128,768]{2,1,0:T(8,128)(2,1)}, bf16[4,128,768]{2,1,0:T(8,128)(2,1)}, f32[4,96,768]{2,1,0:T(8,128)}, f32[96,3072]{1,0:T(8,128)}, f32[384,768]{1,0:T(8,128)}, /*index=5*/f32[8,768]{1,0:T(8,128)}) custom-call(s32[4,4]{1,0:T(4,128)} %len_ref.3, bf16[4,128,768]{2,1,0:T(8,128)(2,1)} %get-tuple-element.37.xrow, ...), custom_call_target="tpu_custom_call" | custom-call | tf_op jit(solution)/shard_map/pallas_call | solution.py:843
  222.3 0.0 copy-start.3
  222.3 2.5 %convert_element_type.6 = f32[4,128,768]{2,1,0:T(8,128)} convert(bf16[4,128,768]{2,1,0:T(8,128)(2,1)} %get-tuple-element.56) | non-fusion elementwise | flops 393216 | bytes 2359296 | tf_op jit(solution)/shard_map/convert_element_type | solution.py:891
  224.8 0.0 copy-done.3
  224.8 1.3 convert_element_type.7
  226.0 0.5 copy-done.2
  226.6 1.0 slice_bitcast_fusion
  227.6 0.8 constant_dynamic-slice_fusion
  228.4 0.5 slice_bitcast_fusion.4
  228.9 0.0 copy-done.1
  228.9 1.0 copy.31
  229.9 0.7 copy-done
  230.6 1.0 copy.32
  (4 shorter events, 0.0 us)
Async XLA Ops:
  4.5 56.6 %copy-start.4 = (f32[768]{0:T(1024)S(1)}, f32[768]{0:T(1024)}, u32[]{:S(2)}) copy-start(f32[768]{0:T(1024)} %param.24) | copy-start | bytes 9220
  4.5 57.2 %copy-start.5 = (f32[768]{0:T(1024)S(1)}, f32[768]{0:T(1024)}, u32[]{:S(2)}) copy-start(f32[768]{0:T(1024)} %param.25) | copy-start | bytes 9220
  222.3 2.5 %copy-start.3 = (bf16[4,128,768]{2,1,0:T(8,128)(2,1)S(1)}, bf16[4,128,768]{2,1,0:T(8,128)(2,1)}, u32[]{:S(2)}) copy-start(bf16[4,128,768]{2,1,0:T(8,128)(2,1)} %get-tuple-element.57) | copy-start | bytes 2359300
  224.8 1.8 copy-start.2
  226.6 2.3 %copy-start.1 = (f32[96,3072]{1,0:T(8,128)S(1)}, f32[96,3072]{1,0:T(8,128)}, u32[]{:S(2)}) copy-start(f32[96,3072]{1,0:T(8,128)} %get-tuple-element.92) | copy-start | bytes 3538948
  228.9 1.7 copy-start

commit v2 on v0

v2 whole, which is shorter than its diff:
```python
import functools

import jax
import jax.numpy as jnp
from jax import lax
from jax.experimental import pallas as pl
from jax.experimental.pallas import tpu as pltpu
from jax.sharding import PartitionSpec as P

CLUSTERS = 100
PAD = 128
EPSILON = 1e-05
GELU_A = 0.7978845608028654
GELU_B = 0.044715
MESH = pl.DeviceIdType.MESH
F32 = jnp.float32
BF16 = jnp.bfloat16
VMEM_LIMIT = 63 * 2**20


def schedule():
    def both(g, *ks):
        return [("one", g, k, o) for k in ks for o in range(2)]

    def side(g, o, *ks):
        return [("one", g, k, o) for k in ks]

    def two(g):
        return [("two", g, k) for k in range(4)]

    return (
        ((),) * 6,
        (both(0, 0), both(0, 1), side(1, 0, 0, 1), side(1, 0, 2, 3), both(0, 2), ()),
        (both(0, 3), side(1, 1, 0, 1), side(1, 1, 2, 3)),
        [("part", 2), ("part", 0)],
        two(0) + two(1) + [("vec", 1)] + both(2, 0, 1, 2, 3) + [("vec", 2)] + two(2)
        + [("three", 0), ("three", 1), ("gather", 0), ("gather", 1), ("vec", 3), ("three", 2), ("gather", 2)],
    )


class Plan:
    def __init__(self, mesh_shape, inputs, clusters, lengths, w_up):
        self.seq, self.dp = mesh_shape["seq"], mesh_shape["dp"]
        self.rows, self.part, self.width = inputs.shape
        self.heads, self.docs, self.hidden = clusters.shape[2], lengths.shape[1], w_up.shape[1]
        self.head = self.width // self.heads
        self.tokens = self.rows * self.part
        self.mates = self.seq // self.rows
        self.sent_docs = 1 if self.mates == 2 else self.docs
        self.block = self.width // self.seq
        self.fast = (
            self.dp == 4 and self.seq == 8 and self.block % 16 == 0 and self.hidden == 4 * self.width
        )
        self.reduce = self.fast
        self.sent_rows = -(-CLUSTERS // 16) * 16
        self.small_rows = 8 if self.mates == 2 else 16
        self.count_rows = -(-self.heads // 8) * 8
        self.tasks = schedule()
        self.square = (self.seq, self.block, self.width) if self.fast else (self.width, self.width)
        self.y_first = ((True,) * 4, (False,) * 4, (True, False, True, False))

    def place(self, j):
        return lax.rem(j, self.rows), j // self.rows

    def owner(self, r, h):
        return h * self.rows + r


def nn(a, b):
    return lax.dot_general(a, b, (((1,), (0,)), ((), ())), preferred_element_type=F32)


def nt(a, b):
    return lax.dot_general(a, b, (((1,), (1,)), ((), ())), preferred_element_type=F32)


def tn(a, b):
    return lax.dot_general(a, b, (((0,), (0,)), ((), ())), preferred_element_type=F32)


def remote(src, dst, send, recv, to):
    return pltpu.make_async_remote_copy(
        src_ref=src, dst_ref=dst, send_sem=send, recv_sem=recv, device_id=to, device_id_type=MESH
    )


def one_hot(row):
    ids = lax.broadcasted_iota(jnp.int32, (PAD, row.shape[1]), 0)
    return jnp.where(ids == row, 1.0, 0.0).astype(BF16)


def doc_masks(z, r, h, len_ref):
    pos = h * z.tokens + lax.broadcasted_iota(jnp.int32, (1, z.tokens), 1)
    seg = jnp.zeros((1, z.tokens), jnp.int32)
    end, ends = jnp.int32(0), []
    for s in range(z.docs):
        end = end + len_ref[r, s]
        ends.append(end)
        seg = seg + (pos >= end).astype(jnp.int32)
    last = sum((z.tokens - 1 >= e).astype(jnp.int32) for e in ends)
    first = sum((z.tokens >= e).astype(jnp.int32) for e in ends)
    spans = last == first
    mine = jnp.where(h == 0, last, first)
    return seg, spans, mine


def stacked_masks(z, seg):
    ids = lax.broadcasted_iota(jnp.int32, (z.docs * z.head, z.tokens), 0)
    body = jnp.where(ids // z.head == seg, 1.0, 0.0).astype(BF16)
    low = lax.broadcasted_iota(jnp.int32, (16, z.tokens), 0)
    tail = jnp.where((low % z.docs == seg) & (low < 2 * z.docs), 1.0, 0.0).astype(BF16)
    return body, tail


def pick_doc(z, blocks, mine):
    out = blocks[0]
    for s in range(1, z.docs):
        out = jnp.where(mine == s, blocks[s], out)
    return out


def mate_id(z, r, h, step):
    return {"seq": z.owner(r, lax.rem(h + step, z.mates))}


def rows_out(z, j, r, h, src, dst, send, recv):
    for row in range(z.rows):
        to = z.owner(row, h)

        @pl.when(to != j)
        def _():
            remote(src.at[row], dst.at[r], send.at[row], recv.at[r], {"seq": to}).start()

        @pl.when(to == j)
        def _():
            pltpu.make_async_copy(src.at[row], dst.at[r], recv.at[r]).start()


def rows_landed(z, j, h, src, dst, send, recv, slot):
    source = z.owner(slot, h)

    @pl.when(source == j)
    def _():
        pltpu.make_async_copy(src.at[0], dst.at[slot], recv.at[slot]).wait()

    @pl.when(source != j)
    def _():
        remote(src.at[0], dst.at[slot], send.at[0], recv.at[slot], {"seq": source}).wait_recv()


def rows_sent(z, j, h, src, dst, send, recv):
    for row in range(z.rows):
        to = z.owner(row, h)

        @pl.when(to != j)
        def _():
            remote(src.at[row], dst.at[0], send.at[row], recv.at[0], {"seq": to}).wait_send()


def norm_parts(values):
    average = jnp.mean(values, axis=-1, keepdims=True)
    centered = values - average
    inverse = lax.rsqrt(jnp.mean(centered * centered, axis=-1, keepdims=True) + EPSILON)
    return centered * inverse, inverse


def norm_back(grad, unit, inverse, gain):
    scaled = grad * gain
    inner = (
        scaled
        - jnp.mean(scaled, axis=-1, keepdims=True)
        - unit * jnp.mean(scaled * unit, axis=-1, keepdims=True)
    )
    return inner * inverse


def joined_masks(z, blocks, seg):
    out = blocks[: z.head]
    for s in range(1, z.docs):
        out = jnp.where(seg == s, blocks[s * z.head : (s + 1) * z.head], out)
    return out


class Refs:
    def __init__(self, names, values):
        self.__dict__.update(zip(names, values, strict=True))


def block_kernel(z, names, *values):
    f = Refs(names, values)
    j = lax.axis_index("seq")
    me = lax.axis_index("dp")
    r, h = z.place(j)
    width, part = z.width, z.part

    barrier = pltpu.get_barrier_semaphore()
    for d in range(1, z.seq):
        pl.semaphore_signal(
            barrier, 1, device_id={"seq": lax.rem(j + d, z.seq)}, device_id_type=MESH
        )
    greeted = z.seq - 1
    if z.reduce:
        for d in range(1, z.dp):
            pl.semaphore_signal(
                barrier, 1, device_id={"dp": lax.rem(me + d, z.dp)}, device_id_type=MESH
            )
        greeted += z.dp - 1

    loads = [
        pltpu.make_async_copy(ref, f.w_qkv.at[p], f.load.at[p])
        for p, ref in enumerate((f.wq_in, f.wk_in, f.wv_in))
    ]
    loads.append(pltpu.make_async_copy(f.wo_in, f.w_o, f.load.at[3]))
    chunks = z.hidden // width
    for c in range(chunks):
        loads.append(
            pltpu.make_async_copy(
                f.up_in.at[(slice(None),) * (len(z.square) - 1) + (pl.ds(c * width, width),)],
                f.w_up.at[c],
                f.load.at[4 + c],
            )
        )
        loads.append(
            pltpu.make_async_copy(f.down_in.at[c], f.w_down.at[c], f.load.at[4 + chunks + c])
        )
    for copy in loads[:3]:
        copy.start()

    seg, spans, mine = doc_masks(z, r, h, f.lengths)
    body_value, tail = stacked_masks(z, seg)
    f.body[...] = body_value
    gain_attn, bias_attn = f.gain_attn[...].reshape(1, width), f.bias_attn[...].reshape(1, width)
    gain_ffn, bias_ffn = f.gain_ffn[...].reshape(1, width), f.bias_ffn[...].reshape(1, width)
    pl.semaphore_wait(barrier, greeted)

    def clu_copy(step):
        to = {"seq": z.owner(lax.rem(r + step, z.rows), h)}
        return remote(f.clu_in, f.clu_got.at[step], f.i_send.at[step], f.i_recv.at[step], to)

    own_clu = pltpu.make_async_copy(f.clu_in, f.clu_got.at[0], f.i_recv.at[0])
    own_clu.start()
    for step in range(1, z.rows):
        clu_copy(step).start()
    rows_out(z, j, r, h, f.x_in, f.xrow, f.x_send, f.x_recv)
    for copy in loads[3:]:
        copy.start()

    def part_rows(t):
        return pl.ds(pl.multiple_of(t * part, part), part)

    def head_rows(i):
        return pl.ds(pl.multiple_of(i * z.head, z.head), z.head)

    own_clu.wait()
    for step in range(z.rows):
        if step:
            clu_copy(step).wait()
        slot = lax.rem(r + z.rows - step, z.rows)
        numbers = f.clu_got[step, :, pl.ds(r, 1), :].reshape(z.heads, part)
        f.clus[:, part_rows(slot)] = numbers

    def mate_copy(src, dst, send, recv, i, step):
        to = {"seq": z.owner(r, lax.rem(h + step, z.mates))}
        return remote(src.at[i], dst.at[step - 1, i], send.at[step - 1, i], recv.at[step - 1, i], to)

    def sum_copy(i, step):
        return mate_copy(f.sums, f.sums_in, f.a_ss, f.a_rs, i, step)

    def result_copies(i, step):
        return (
            mate_copy(f.big, f.big_in, f.b_ss, f.b_rs, i, step),
            mate_copy(f.small, f.small_in, f.s_ss, f.s_rs, i, step),
        )

    def grad_copy(i, step):
        return mate_copy(f.g_send, f.g_recv, f.g_ss, f.g_rs, i, step)

    def cent_copy(i, step):
        return mate_copy(f.c_s, f.c_got, f.q_ss, f.q_rs, i, step)

    others = range(1, z.mates)
    stack = z.docs * z.head
    pairs = z.heads // 2
    low_lanes = z.sent_rows

    def pack(pair):
        return pair.astype(BF16).T[:low_lanes]

    def unpack(packed):
        rest = jnp.zeros((PAD - low_lanes, PAD), BF16)
        return jnp.concatenate([packed, rest], axis=0).T.astype(F32)

    def member_of(i):
        return one_hot(f.clus[pl.ds(i, 1), :])

    ones = jnp.ones((8, z.tokens), BF16)
    f.cnt_out[...] = jnp.zeros_like(f.cnt_out)
    for i in range(z.heads):
        f.cnt_out[i : i + 1] = nt(ones, one_hot(f.clus[i : i + 1, :]))[:1]

    def count_copy(step):
        to = {"seq": z.owner(r, lax.rem(h + step, z.mates))}
        return remote(f.cnt_out, f.cnt_in.at[step - 1], f.k_ss.at[step - 1], f.k_rs.at[step - 1], to)

    for step in others:
        count_copy(step).start()
    for copy in loads[:3]:
        copy.wait()

    def project(slot, carry):
        rows_landed(z, j, h, f.x_in, f.xrow, f.x_send, f.x_recv, slot)
        unit, _ = norm_parts(f.xrow[slot].astype(F32))
        normed = (unit * gain_attn + bias_attn).astype(BF16)
        f.low[part_rows(slot), :] = normed
        f.n_t[:, part_rows(slot)] = normed.T
        f.q_t[:, part_rows(slot)] = nn(normed, f.w_qkv[0]).astype(BF16).T
        return carry

    lax.fori_loop(0, z.rows, project, 0)

    def cluster_sums(i, carry):
        pair = jnp.concatenate(
            [nt(f.q_t[head_rows(2 * i + a), :], member_of(2 * i + a)) for a in range(2)], axis=0
        )
        f.sums_f[i] = pair
        f.sums[i] = pack(pair)
        for step in others:
            sum_copy(i, step).start()
        return carry

    lax.fori_loop(0, pairs, cluster_sums, 0)
    rows_sent(z, j, h, f.x_in, f.xrow, f.x_send, f.x_recv)
    rows_out(z, j, r, h, f.c_in, f.crow, f.c_send, f.c_recv)
    counts = f.cnt_out[...]
    for step in others:
        count_copy(step).wait()
        counts = counts + f.cnt_in[step - 1]
    f.cnts[...] = jnp.maximum(counts, 1.0)

    def project_more(t, carry):
        normed = f.low[part_rows(t), :]
        f.k_t[:, part_rows(t)] = nn(normed, f.w_qkv[1]).astype(BF16).T
        f.v_t[:, part_rows(t)] = nn(normed, f.w_qkv[2]).astype(BF16).T
        return carry

    lax.fori_loop(0, z.rows, project_more, 0)

    def masked_values(i):
        return jnp.concatenate([f.v_t[head_rows(i), :]] * z.docs, axis=0) * f.body[...]

    def doc_rows(blocks, s):
        return blocks[s * z.head : (s + 1) * z.head]

    def border(blocks):
        if z.mates == 2:
            parts = [[doc_rows(b, s) for s in range(z.docs)] for b in blocks]
            return [pack(jnp.concatenate([pick_doc(z, p, mine) for p in parts], axis=0))]
        return [
            pack(jnp.concatenate([doc_rows(b, s) for b in blocks], axis=0)) for s in range(z.docs)
        ]

    def attend(i, carry):
        total = f.sums_f[i]
        for step in others:
            sum_copy(i, step).wait()
            total = total + unpack(f.sums_in[step - 1, i])
        blocks, small = [], []
        for a in range(2):
            n = 2 * i + a
            count = f.cnts[pl.ds(n, 1), :]
            cent = (total[a * z.head : (a + 1) * z.head] / count).astype(BF16)
            f.cent_t[n] = cent
            scores = tn(cent, f.k_t[head_rows(n), :]) * 0.125
            top = jnp.max(scores, axis=1, keepdims=True)
            weights = jnp.exp(scores - top).astype(BF16)
            f.wts[n] = weights
            both = nt(jnp.concatenate([masked_values(n), tail], axis=0), weights)
            f.u_s[n] = both[:stack]
            top_row = jnp.broadcast_to(top, (PAD, PAD)).T
            denoms = both[stack : stack + 4]
            f.dens[n] = jnp.concatenate([denoms, top_row[:4]], axis=0)
            blocks.append(both[:stack])
            if z.mates == 2:
                own = pick_doc(z, [denoms[s : s + 1] for s in range(z.docs)], mine)
                small += [jnp.broadcast_to(own, (2, PAD)), top_row[:2]]
            else:
                small += [denoms, top_row[:4]]
        f.small[i] = jnp.concatenate(small, axis=0)
        for d, packed in enumerate(border(blocks)):
            f.big[i, d] = packed
        for step in others:
            for copy in result_copies(i, step):
                copy.start()
        return carry

    lax.fori_loop(0, pairs, attend, 0)
    empty = [jnp.where(jnp.sum((seg == s).astype(F32)) > 0.5, 0.0, 1.0) for s in range(z.docs)]
    half_small = z.small_rows // 2

    def finish(i, carry):
        got = []
        for step in others:
            for copy in result_copies(i, step):
                copy.wait()
            got.append([unpack(f.big_in[step - 1, i, d]) for d in range(z.sent_docs)])
        for a in range(2):
            n = 2 * i + a
            own = f.dens[n]
            top, highest = own[4:5], own[4:5]
            sides = []
            for step in others:
                side = f.small_in[step - 1, i, a * half_small : (a + 1) * half_small]
                sides.append((side, side[half_small // 2 : half_small // 2 + 1]))
                highest = jnp.maximum(highest, sides[-1][1])
            scale = jnp.exp(top - highest)
            scaled, factors = [], []
            for s in range(z.docs):
                piece = f.u_s[n, s * z.head : (s + 1) * z.head]
                denom = own[s : s + 1]
                joined, joined_denom = piece * scale, denom * scale
                d = 0 if z.mates == 2 else s
                for other, (side, side_top) in zip(got, sides):
                    side_scale = jnp.exp(side_top - highest)
                    joined = joined + other[d][a * z.head : (a + 1) * z.head] * side_scale
                    joined_denom = joined_denom + side[d : d + 1] * side_scale
                here = jnp.logical_and(spans, mine == s) if z.mates == 2 else True
                joined = jnp.where(here, joined, piece)
                joined_denom = jnp.where(here, joined_denom, denom)
                factor = jnp.where(here, scale, jnp.ones_like(scale))
                joined_denom = joined_denom + jnp.where(joined_denom > 0.0, 0.0, empty[s])
                inverse = 1.0 / joined_denom
                scaled.append((joined * inverse).astype(BF16))
                factors.append(inverse * factor)
            result = jnp.concatenate(scaled, axis=0)
            f.res_t[n] = result
            f.rfac[n] = jnp.concatenate(factors + [jnp.zeros((8 - z.docs, PAD), F32)], axis=0)
            f.att_t[head_rows(n), :] = joined_masks(z, nn(result, member_of(n)), seg).astype(BF16)
        return carry

    lax.fori_loop(0, pairs, finish, 0)

    core, y = lax.rem(me, 2), me // 2
    xx, zz = lax.rem(j, 2), j // 2
    sibling, across = me + 1 - 2 * core, me + 2 - 4 * y
    beside = j + 1 - 2 * xx
    deep = z.seq // 2
    if z.reduce:
        grads = (f.d_down, f.d_up, f.w_up)
        core_in = (f.core_in.at[0], f.core_in.at[1], f.w_down.at[pl.ds(0, 2)])
        first_in = (f.first_in.at[0], f.first_in.at[1], f.w_down.at[2])

    def add(ref, value):
        ref[...] = (ref[...].astype(F32) + value.astype(F32)).astype(BF16)

    def block(g, yp, xb, k):
        return core_in[g].at[yp, 2 * k + xb]

    def grad_block(g, p, b):
        return grads[g][p, b]

    def down_core(yp, c):
        src = f.d_down.at[yp * 2 + 1 - core, pl.ds(2 * c, 2)]
        dst = core_in[0].at[yp, pl.ds(2 * c, 2)]
        return remote(src, dst, f.dn_ss.at[yp, c], f.dn_rs.at[yp, c], {"dp": sibling})

    def part_core(g, p):
        yp = p // 2
        if g == 1:
            src, dst = f.d_up.at[p], core_in[1].at[yp]
        else:
            src, dst = f.w_up.at[p], f.w_down.at[yp]
        return remote(src, dst, f.co_ss.at[g - 1, yp], f.co_rs.at[g - 1, yp], {"dp": sibling})

    def y_first(g, k):
        return z.y_first[g][k]

    def step_one(g, k, other):
        if y_first(g, k):
            src, to = block(g, 1 - y, other, k), {"dp": across}
        else:
            src, to = block(g, other, 1 - xx, k), {"seq": beside}
        dst = first_in[g].at[other * deep + k]
        return remote(src, dst, f.f_ss.at[g, other, k], f.f_rs.at[g, other, k], to)

    def step_two(g, k):
        if y_first(g, k):
            src, to = block(g, y, 1 - xx, k), {"seq": beside}
        else:
            src, to = block(g, 1 - y, xx, k), {"dp": across}
        return remote(src, f.second_in.at[g, k], f.n_ss.at[g, k], f.n_rs.at[g, k], to)

    def one_done(g, k, other):
        if y_first(g, k):
            own, far = block(g, y, other, k), xx != other
        else:
            own, far = block(g, other, xx, k), y != other
        step_one(g, k, other).wait_recv()
        add(own, first_in[g][other * deep + k])
        pl.when(far)(lambda: step_two(g, k).start())

    def step_three(g, k):
        return remote(
            block(g, y, xx, k), f.third_in.at[g, zz], f.t_ss.at[g, k], f.t_rs.at[g, zz],
            {"seq": 2 * k + xx},
        )

    def two_done(g, k):
        step_two(g, k).wait_recv()
        add(block(g, y, xx, k), f.second_in[g, k])

        @pl.when(zz != k)
        def _():
            step_three(g, k).start()

    def gather_copy(g, kind):
        src = across if kind == 2 else me
        to = {"dp": across if kind == 1 else sibling}
        ref = f.gat.at[g, src]
        return remote(ref, ref, f.w_ss.at[g, kind], f.w_rs.at[g, kind], to)

    def three_done(g):
        total = core_in[g][y, j].astype(F32)
        for k in range(1, deep):
            source = lax.rem(zz + k, deep)
            remote(
                block(g, y, xx, zz), f.third_in.at[g, source], f.t_ss.at[g, source],
                f.t_rs.at[g, source], {"seq": 2 * source + xx},
            ).wait_recv()
            total = total + f.third_in[g, source].astype(F32)
        f.gat[g, me] = total.astype(BF16)
        gather_copy(g, 1).start()
        gather_copy(g, 0).start()

    def gather_wait(g, kind):
        source = (sibling, across, across + sibling - me)[kind]
        ref = f.gat.at[g, source]
        to = {"dp": across if kind == 1 else sibling}
        remote(ref, ref, f.w_ss.at[g, kind], f.w_rs.at[g, kind], to).wait_recv()

    def gather_done(g):
        gather_wait(g, 1)
        gather_copy(g, 2).start()

    def part_done(g, p):
        yp = p // 2
        part_core(g, p).wait_recv()

        def body(b, carry):
            add(core_in[g].at[yp, b], grad_block(g, p, b))
            return carry

        lax.fori_loop(0, z.seq, body, 0)
        for k in range(deep):
            if y_first(g, k):

                @pl.when(yp != y)
                def _():
                    step_one(g, k, 1 - xx).start()
                    step_one(g, k, xx).start()
            else:
                step_one(g, k, yp).start()

    def down_done(c):
        for yp in range(2):
            down_core(yp, c).wait_recv()
            for xb in range(2):
                add(block(0, yp, xb, c), f.d_down[yp * 2 + core, 2 * c + xb])
            if y_first(0, c):

                @pl.when(yp != y)
                def _():
                    step_one(0, c, 1 - xx).start()
                    step_one(0, c, xx).start()
            else:
                step_one(0, c, yp).start()

    def core_done(c):
        down_done(c)
        pl.when(c % 2 == core)(lambda: part_done(1, c))

    def vec_copy(t, to):
        return remote(f.vec_buf.at[min(t, 2)], f.vec_got.at[t], f.v_ss.at[t], f.v_rs.at[t], to)

    def vec_step(t):
        if t == 1:
            vec_copy(0, {"dp": sibling}).wait()
            f.vec_buf[1] = f.vec_buf[0] + f.vec_got[0]
            vec_copy(1, {"dp": across}).start()
            return
        if t == 2:
            vec_copy(1, {"dp": across}).wait()
            f.vec_buf[2] = f.vec_buf[1] + f.vec_got[1]
        total = f.vec_buf[2]
        for d in range(1, z.seq):
            copy = vec_copy(1 + d, {"seq": lax.rem(j + d, z.seq)})
            if t == 2:
                copy.start()
            else:
                copy.wait()
                total = total + f.vec_got[1 + d]
        if t == 3:
            f.vec_ref[...] = total

    def part_step(which):
        for p in range(2):
            pl.when(core == p)(lambda p=p: part_done(2, p + which))

    steps = {
        "one": one_done, "two": two_done, "three": three_done, "gather": gather_done,
        "vec": vec_step, "part": part_step,
    }

    def run(tasks):
        for name, *numbers in tasks:
            steps[name](*numbers)

    def serve(i, table):
        if z.reduce:
            for at, tasks in enumerate(table):
                if tasks:
                    pl.when(i == at)(functools.partial(run, tasks))

    for copy in loads[3:]:
        copy.wait()

    def first(t, carry):
        rows = part_rows(t)
        middle = f.xrow[t].astype(F32) + tn(f.att_t[:, rows], f.w_o[...])
        f.acc[rows, :] = middle
        f.gm[rows, :] = middle
        unit, _ = norm_parts(middle)
        normed = (unit * gain_ffn + bias_ffn).astype(BF16)
        f.low[rows, :] = normed
        f.low_t[:, rows] = normed.T
        f.acc_n[rows, :] = jnp.zeros((part, width), F32)
        return carry

    lax.fori_loop(0, z.rows, first, 0)
    for slot in range(z.rows):
        rows_landed(z, j, h, f.c_in, f.crow, f.c_send, f.c_recv, slot)
    rows_sent(z, j, h, f.c_in, f.crow, f.c_send, f.c_recv)
    halves = z.rows // 2

    def chunk(c, carry):
        w_up, w_down = f.w_up[c].reshape(width, width), f.w_down[c].reshape(width, width)
        for t in range(2):
            rows = slice(t * halves * part, (t + 1) * halves * part)
            own = slice(t * halves, (t + 1) * halves)
            grad_out = f.crow[own].reshape(halves * part, width)
            u = nn(f.low[rows, :], w_up)
            tanh = jnp.tanh(GELU_A * (u + GELU_B * (u * u * u)))
            cdf = 0.5 * (1.0 + tanh)
            f.act[own] = (u * cdf).astype(BF16).reshape(halves, part, width)
            slope = cdf + (0.5 * GELU_A) * u * (1.0 - tanh * tanh) * (1.0 + (3.0 * GELU_B) * (u * u))
            grad = nt(grad_out, w_down)
            f.gp[own] = (grad * slope).astype(BF16).reshape(halves, part, width)
            f.acc[rows, :] += nn(f.act[own].reshape(halves * part, width), w_down)
            f.acc_n[rows, :] += nt(f.gp[own].reshape(halves * part, width), w_up)
            if z.reduce and t == 0 and c:
                core_done(c - 1)
        down = tn(
            f.act[...].reshape(z.tokens, width), f.crow[...].reshape(z.tokens, width)
        ).astype(BF16)
        if z.fast:
            for b in range(2):
                for p in range(z.dp):
                    at = (b * z.dp + p) * z.block
                    f.d_down[p, 2 * c + b] = down[at : at + z.block]
        else:
            f.d_down[pl.ds(pl.multiple_of(c * width, width), width), :] = down
        if z.reduce:
            for yp in range(2):
                down_core(yp, c).start()
        up = nn(f.low_t[...], f.gp[...].reshape(z.tokens, width)).astype(BF16)
        f.d_up[c] = up.reshape(f.d_up.shape[1:])
        if z.reduce:
            pl.when(c % 2 != core)(lambda: part_core(1, c).start())
        return carry

    if z.reduce:
        for c in range(chunks):
            chunk(c, 0)
    else:
        lax.fori_loop(0, chunks, chunk, 0)

    def ffn_back(t, carry):
        rows = part_rows(t)
        f.act[t] = f.acc[rows, :].astype(BF16)
        unit, inverse = norm_parts(f.gm[rows, :])
        grad = f.acc_n[rows, :]
        grad_middle = f.crow[t].astype(F32) + norm_back(grad, unit, inverse, gain_ffn)
        f.gm[rows, :] = grad_middle
        f.low[rows, :] = grad_middle.astype(BF16)
        return (
            carry[0] + jnp.sum(grad * unit, axis=0, keepdims=True),
            carry[1] + jnp.sum(grad, axis=0, keepdims=True),
        )

    zero = jnp.zeros((1, width), F32)
    sums_ffn = lax.fori_loop(0, z.rows, ffn_back, (zero, zero))
    rows_out(z, j, r, h, f.act, f.out_ref, f.o_send, f.o_recv)
    f.ga_t[...] = nt(f.w_o[...], f.low[...]).astype(BF16)

    if z.reduce:
        core_done(chunks - 1)

    def gather_grads(i, carry):
        blocks = []
        for a in range(2):
            n = 2 * i + a
            masked = jnp.concatenate([f.ga_t[head_rows(n), :]] * z.docs, axis=0) * f.body[...]
            blocks.append(nt(masked, member_of(n)))
            f.u_s[n] = blocks[-1]
        for d, packed in enumerate(border(blocks)):
            f.g_send[i, d] = packed
        for step in others:
            grad_copy(i, step).start()
        serve(i, z.tasks[0])
        return carry

    lax.fori_loop(0, pairs, gather_grads, 0)
    f.w_up[3] = nn(f.att_t[...], f.low[...]).astype(BF16).reshape(z.square)
    if z.reduce:
        pl.when(core == 0)(lambda: part_core(2, 3).start())

    def attend_back(i, carry):
        serve(i, z.tasks[1])
        got = []
        for step in others:
            grad_copy(i, step).wait()
            got.append([unpack(f.g_recv[step - 1, i, d]) for d in range(z.sent_docs)])
        cents = []
        for a in range(2):
            n = 2 * i + a
            result, factor = f.res_t[n], f.rfac[n]
            lows, deltas = [], []
            for s in range(z.docs):
                grad = f.u_s[n, s * z.head : (s + 1) * z.head]
                joined = grad
                for other in got:
                    piece = other[0 if z.mates == 2 else s]
                    joined = joined + piece[a * z.head : (a + 1) * z.head]
                if z.mates == 2:
                    joined = jnp.where(jnp.logical_and(spans, mine == s), joined, grad)
                scaled = joined * factor[s : s + 1]
                lows.append(scaled.astype(BF16))
                piece = doc_rows(result, s).astype(F32)
                deltas.append(-jnp.sum(scaled * piece, axis=0, keepdims=True))
            delta = jnp.concatenate(deltas, axis=0)
            high = delta.astype(BF16).astype(F32)
            small = jnp.concatenate(
                [high, delta - high, jnp.zeros((16 - 2 * z.docs, PAD), F32)], axis=0
            ).astype(BF16)
            low = jnp.concatenate(lows, axis=0)
            diff = tn(
                jnp.concatenate([low, small], axis=0),
                jnp.concatenate([masked_values(n), tail], axis=0),
            )
            weights = f.wts[n]
            raw = (0.125 * (weights.astype(F32) * diff)).astype(BF16)
            f.gk_t[head_rows(n), :] = nn(f.cent_t[n], raw).astype(BF16)
            f.gv_t[head_rows(n), :] = joined_masks(z, nn(low, weights), seg).astype(BF16)
            cents.append(nt(f.k_t[head_rows(n), :], raw))
        pair = jnp.concatenate(cents, axis=0)
        f.c_f[i] = pair
        f.c_s[i] = pack(pair)
        for step in others:
            cent_copy(i, step).start()
        return carry

    lax.fori_loop(0, pairs, attend_back, 0)

    def weight_grad(p, g_ref):
        f.w_up[p] = nt(f.n_t[...], g_ref[...]).astype(BF16).reshape(z.square)
        if z.reduce:
            pl.when(p % 2 != core)(lambda: part_core(2, p).start())

    weight_grad(1, f.gk_t)
    weight_grad(2, f.gv_t)

    def query_back(i, carry):
        total = f.c_f[i]
        for step in others:
            cent_copy(i, step).wait()
            total = total + unpack(f.c_got[step - 1, i])
        for a in range(2):
            n = 2 * i + a
            low = (total[a * z.head : (a + 1) * z.head] / f.cnts[pl.ds(n, 1), :]).astype(BF16)
            f.q_t[head_rows(n), :] = nn(low, member_of(n)).astype(BF16)
        serve(i, z.tasks[2])
        return carry

    lax.fori_loop(0, pairs, query_back, 0)
    weight_grad(0, f.q_t)

    if z.reduce:
        run(z.tasks[3])

    total = (
        nn(f.w_qkv[0], f.q_t[...]) + nn(f.w_qkv[1], f.gk_t[...]) + nn(f.w_qkv[2], f.gv_t[...])
    )
    f.acc[...] = total.T

    def attn_back(t, carry):
        rows = part_rows(t)
        unit, inverse = norm_parts(f.xrow[t].astype(F32))
        grad = f.acc[rows, :]
        f.gp[t] = (f.gm[rows, :] + norm_back(grad, unit, inverse, gain_attn)).astype(BF16)
        return (
            carry[0] + jnp.sum(grad * unit, axis=0, keepdims=True),
            carry[1] + jnp.sum(grad, axis=0, keepdims=True),
        )

    sums_attn = lax.fori_loop(0, z.rows, attn_back, (zero, zero))
    rows_out(z, j, r, h, f.gp, f.gx_ref, f.y_send, f.y_recv)
    vectors = jnp.concatenate([*sums_attn, *sums_ffn, jnp.zeros((4, width), F32)], axis=0)

    if z.reduce:
        f.vec_buf[0] = vectors
        vec_copy(0, {"dp": sibling}).start()
        run(z.tasks[4])
        for g in range(3):
            gather_wait(g, 0)
            gather_wait(g, 2)
            for kind in range(3):
                gather_copy(g, kind).wait_send()
            for k in range(deep):
                for other in range(2):
                    step_one(g, k, other).wait_send()
                step_two(g, k).wait_send()

                @pl.when(zz != k)
                def _():
                    step_three(g, k).wait_send()

        for yp in range(2):
            for c in range(chunks):
                down_core(yp, c).wait_send()
            for g in (1, 2):
                part_core(g, yp * 2 + 1 - core).wait_send()
    else:
        f.vec_ref[...] = vectors
        if not z.fast:
            copy = pltpu.make_async_copy(f.w_up, f.d_qkvo, f.load.at[0])
            copy.start()
            copy.wait()

    for slot in range(z.rows):
        rows_landed(z, j, h, f.act, f.out_ref, f.o_send, f.o_recv, slot)
        rows_landed(z, j, h, f.gp, f.gx_ref, f.y_send, f.y_recv, slot)
    rows_sent(z, j, h, f.act, f.out_ref, f.o_send, f.o_recv)
    rows_sent(z, j, h, f.gp, f.gx_ref, f.y_send, f.y_recv)


def local(
    mesh_shape,
    inputs, cotangent, lengths, clusters, gain_attn, bias_attn, w_query, w_key, w_value, w_out,
    gain_ffn, bias_ffn, w_up, w_down,
):
    z = Plan(mesh_shape, inputs, clusters, lengths, w_up)
    width, tokens, heads, docs = z.width, z.tokens, z.heads, z.docs
    others, stack, chunks = z.mates - 1, z.docs * z.head, z.hidden // z.width
    anywhere = pl.BlockSpec(memory_space=pl.ANY)
    vmem = pl.BlockSpec(memory_space=pltpu.VMEM)
    smem = pl.BlockSpec(memory_space=pltpu.SMEM)
    dma = pltpu.SemaphoreType.DMA
    shape = jax.ShapeDtypeStruct
    turned = jnp.transpose(clusters, (2, 0, 1))
    rows = (z.rows, z.part, width)

    ins = [
        ("x_in", inputs, anywhere), ("c_in", cotangent, anywhere), ("clu_in", turned, anywhere),
        ("lengths", lengths, smem), ("gain_attn", gain_attn, vmem), ("bias_attn", bias_attn, vmem),
        ("gain_ffn", gain_ffn, vmem), ("bias_ffn", bias_ffn, vmem),
        ("wq_in", w_query, anywhere), ("wk_in", w_key, anywhere), ("wv_in", w_value, anywhere),
        ("wo_in", w_out, anywhere), ("up_in", w_up.reshape(z.square[:-1] + (z.hidden,)), anywhere),
        ("down_in", w_down.reshape((chunks,) + z.square), anywhere),
    ]
    outs = [
        ("out_ref", shape(rows, BF16), anywhere), ("gx_ref", shape(rows, BF16), anywhere),
        ("vec_ref", shape((8, width), F32), vmem),
    ]
    pairs, packed = heads // 2, (z.sent_rows, PAD)
    scratch = [
        ("w_qkv", (3, width, width), BF16), ("w_o", (width, width), BF16),
        ("w_up", (chunks,) + z.square, BF16), ("w_down", (chunks,) + z.square, BF16),
        ("xrow", rows, BF16), ("crow", rows, BF16),
        ("clu_got", (z.rows, heads, z.rows, z.part), jnp.int32), ("clus", (heads, tokens), jnp.int32),
        ("n_t", (width, tokens), BF16), ("q_t", (width, tokens), BF16),
        ("k_t", (width, tokens), BF16), ("v_t", (width, tokens), BF16),
        ("att_t", (width, tokens), BF16), ("wts", (heads, PAD, tokens), BF16),
        ("cent_t", (heads, z.head, PAD), BF16), ("cnts", (z.count_rows, PAD), F32), ("cnt_out", (z.count_rows, PAD), F32),
        ("cnt_in", (others, z.count_rows, PAD), F32), ("dens", (heads, 8, PAD), F32),
        ("res_t", (heads, stack, PAD), BF16), ("rfac", (heads, 8, PAD), F32),
        ("u_s", (heads, stack, PAD), F32), ("body", (stack, tokens), BF16),
        ("sums_f", (pairs, PAD, PAD), F32),
        ("sums", (pairs,) + packed, BF16), ("sums_in", (others, pairs) + packed, BF16),
        ("big", (pairs, z.sent_docs) + packed, BF16),
        ("big_in", (others, pairs, z.sent_docs) + packed, BF16),
        ("small", (pairs, z.small_rows, PAD), F32), ("small_in", (others, pairs, z.small_rows, PAD), F32),
        ("g_send", (pairs, z.sent_docs) + packed, BF16),
        ("g_recv", (others, pairs, z.sent_docs) + packed, BF16),
        ("c_f", (pairs, PAD, PAD), F32), ("c_s", (pairs,) + packed, BF16),
        ("c_got", (others, pairs) + packed, BF16),
        ("low", (tokens, width), BF16), ("low_t", (width, tokens), BF16),
        ("act", rows, BF16), ("gp", rows, BF16),
        ("acc", (tokens, width), F32), ("acc_n", (tokens, width), F32), ("gm", (tokens, width), F32),
        ("ga_t", (width, tokens), BF16), ("gk_t", (width, tokens), BF16), ("gv_t", (width, tokens), BF16),
    ]
    sems = [("load", (4 + 2 * chunks,))]
    for n in ("i", "x", "c", "o", "y"):
        sems += [(n + "_send", (z.rows,)), (n + "_recv", (z.rows,))]
    for n in ("a", "b", "s", "g", "q"):
        sems += [(n + "_ss", (others, pairs)), (n + "_rs", (others, pairs))]
    sems += [("k_ss", (others,)), ("k_rs", (others,))]
    if z.fast:
        piece = (z.block, width)
        deep = z.seq // 2
        outs.append(("gat", shape((3, z.dp) + piece, BF16), vmem))
        scratch += [
            ("d_down", (z.dp, z.seq) + piece, BF16), ("d_up", (z.dp, z.seq) + piece, BF16),
            ("core_in", (2, 2, z.seq) + piece, BF16), ("first_in", (2, z.seq) + piece, BF16),
            ("second_in", (3, deep) + piece, BF16), ("third_in", (3, deep) + piece, BF16),
            ("vec_buf", (3, 8, width), F32), ("vec_got", (z.seq + 1, 8, width), F32),
        ]
        sems += [
            ("dn_ss", (2, chunks)), ("dn_rs", (2, chunks)), ("co_ss", (2, 2)), ("co_rs", (2, 2)),
            ("f_ss", (3, 2, deep)), ("f_rs", (3, 2, deep)), ("n_ss", (3, deep)), ("n_rs", (3, deep)),
            ("t_ss", (3, deep)), ("t_rs", (3, deep)), ("w_ss", (3, 3)), ("w_rs", (3, 3)),
            ("v_ss", (z.seq + 1,)), ("v_rs", (z.seq + 1,)),
        ]
    else:
        outs += [
            ("d_qkvo", shape((4, width, width), BF16), anywhere),
            ("d_up", shape((chunks, width, width), BF16), vmem),
            ("d_down", shape((z.hidden, width), BF16), vmem),
        ]
    names = [n for n, _, _ in ins + outs + scratch] + [n for n, _ in sems]
    results = pl.pallas_call(
        functools.partial(block_kernel, z, names),
        out_shape=[s for _, s, _ in outs],
        in_specs=[s for _, _, s in ins],
        out_specs=[s for _, _, s in outs],
        scratch_shapes=[pltpu.VMEM(s, t) for _, s, t in scratch] + [dma(s) for _, s in sems],
        compiler_params=pltpu.CompilerParams(
            collective_id=0, has_side_effects=True, vmem_limit_bytes=VMEM_LIMIT
        ),
    )(*[v for _, v, _ in ins])

    out_back, grad_back, vectors = results[:3]
    if z.fast:
        gat = results[3].astype(F32)
        g_down = gat[0].reshape(-1, width)
        g_up = jnp.transpose(gat[1], (1, 0, 2)).reshape(z.block, -1)
        g_qkvo = gat[2]
        own = lax.dynamic_slice_in_dim(vectors, lax.axis_index("seq") * z.block, z.block, 1)
    else:

        def share(v, dim):
            v = lax.psum_scatter(v.astype(F32), "seq", scatter_dimension=dim, tiled=True)
            return lax.psum(v, "dp")

        g_up = share(jnp.transpose(results[4], (1, 0, 2)).reshape(width, z.hidden), 0)
        g_qkvo, g_down, own = share(results[3], 1), share(results[5], 0), share(vectors, 1)
    return (
        out_back.astype(F32), grad_back.astype(F32), own[0], own[1],
        g_qkvo[0], g_qkvo[1], g_qkvo[2], g_qkvo[3], own[2], own[3], g_up, g_down,
    )


def solution(mesh):
    spread = P("dp", "seq", None)
    return jax.shard_map(
        functools.partial(local, dict(mesh.shape)),
        mesh=mesh,
        in_specs=(spread, spread, P("dp", None), spread) + (P(),) * 10,
        out_specs=(spread, spread, P("seq"), P("seq")) + (P("seq", None),) * 4
        + (P("seq"), P("seq"), P("seq", None), P("seq", None)),
        check_vma=False,
    )
```

time: 1450 us -> 158 us (0.11)
  the two profiles are of different devices: /device:TPU:0 before, /device:TPU:25 now
where the time goes in v2:
time: 158 us
  Pallas kernels  148 us (94%)
  local copies, waits for them, and re-layouts  5.5 us (3%)
  other arithmetic  4.34 us (3%)
    pallas_call x1, Pallas kernels, local(): pl.pallas_call(functools.partial(block_kernel, z, names), out_shape=[s fo...  148 us

profile of v2, /device:TPU:25, one launch (start us, length us, event | category | flops | bytes accessed | tf_op | source)
XLA Modules:
  0.0 158.1 jit_solution(6424724993020018169)
XLA Ops:
  0.7 147.5 %shard_map.229 = (bf16[4,128,768]{2,1,0:T(8,128)(2,1)}, bf16[4,128,768]{2,1,0:T(8,128)(2,1)}, f32[8,768]{1,0:T(8,128)}, bf16[3,4,96,768]{3,2,1,0:T(8,128)(2,1)}) custom-call(bf16[4,128,768]{2,1,0:T(8,128)(2,1)} %values_0_.1, bf16[4,128,768]{2,1,0:T(8,128)(2,1)} %values_1_.1, s32[12,4,128]{2,1,0:T(4,128)} %bitcast.30, s32[4,4]{1,0:T(4,128)} %values_3_.1, ...), custom_call_target="tpu_custom_call" | custom-call | tf_op jit(solution)/shard_map/pallas_call | solution.py:939
  148.2 0.8 constant_dynamic-slice_fusion
  149.0 0.5 slice_bitcast_fusion.5
  149.5 1.8 %convert_element_type.11 = f32[3,4,96,768]{3,2,1,0:T(8,128)S(1)} convert(bf16[3,4,96,768]{3,2,1,0:T(8,128)(2,1)} %get-tuple-element.19) | non-fusion elementwise | flops 884736 | bytes 5308416 | tf_op jit(solution)/shard_map/convert_element_type | solution.py:952
  151.3 1.0 slice_bitcast_fusion.1
  152.3 0.1 slice_bitcast_fusion
  152.4 0.0 copy-start
  152.4 1.1 copy.27
  153.6 0.0 copy-start.2
  153.6 0.8 copy-done
  154.3 1.1 slice.54
  155.4 0.0 copy-start.1
  155.4 0.0 copy-done.2
  155.4 1.3 convert_element_type.10
  156.7 0.1 copy-done.1
  156.8 1.3 convert_element_type.9
Async XLA Ops:
  152.4 1.9 %copy-start = (bf16[3,4,96,768]{3,2,1,0:T(8,128)(2,1)S(1)}, bf16[3,4,96,768]{3,2,1,0:T(8,128)(2,1)}, u32[]{:S(2)}) copy-start(bf16[3,4,96,768]{3,2,1,0:T(8,128)(2,1)} %get-tuple-element.19) | copy-start | bytes 5308420
  153.6 1.9 %copy-start.2 = (bf16[4,128,768]{2,1,0:T(8,128)(2,1)S(1)}, bf16[4,128,768]{2,1,0:T(8,128)(2,1)}, u32[]{:S(2)}) copy-start(bf16[4,128,768]{2,1,0:T(8,128)(2,1)} %get-tuple-element.17) | copy-start | bytes 2359300
  155.4 1.3 copy-start.1

commit v3 on v2

--- a/solution.py
+++ b/solution.py
@@ -13,28 +13,38 @@
 GELU_A = 0.7978845608028654
 GELU_B = 0.044715
 MESH = pl.DeviceIdType.MESH
+YF = ((True, False, True, True), (False, True, False, True), (True, True, True, False))
 F32 = jnp.float32
 BF16 = jnp.bfloat16
 VMEM_LIMIT = 63 * 2**20
 
 
-def schedule():
+def schedule(order):
     def both(g, *ks):
         return [("one", g, k, o) for k in ks for o in range(2)]
 
+    def two(g, *ks):
+        return [("two", g, k) for k in ks]
+
     def side(g, o, *ks):
         return [("one", g, k, o) for k in ks]
 
-    def two(g):
-        return [("two", g, k) for k in range(4)]
-
+    a, b, c, d = order
+    forward = {a: [], b: [("down", a)], c: [("down", b)], d: [("down", c)]}
+    mixed = [step for k in order for step in two(1, k) + both(2, k)]
     return (
+        [forward[k] for k in range(4)],
+        ([("down", d)], [], [("up", 0)] + both(0, a), [("up", 1)] + both(0, b)),
+        [("up", 2)] + both(0, c),
+        ((), (), (), (), (), [("up", 3)]),
+        ((), (), (), (), (), both(0, d)),
         ((),) * 6,
-        (both(0, 0), both(0, 1), side(1, 0, 0, 1), side(1, 0, 2, 3), both(0, 2), ()),
-        (both(0, 3), side(1, 1, 0, 1), side(1, 1, 2, 3)),
-        [("part", 2), ("part", 0)],
-        two(0) + two(1) + [("vec", 1)] + both(2, 0, 1, 2, 3) + [("vec", 2)] + two(2)
-        + [("three", 0), ("three", 1), ("gather", 0), ("gather", 1), ("vec", 3), ("three", 2), ("gather", 2)],
+        both(1, *order),
+        [("part", 3), ("part", 1), ("part", 2), ("part", 0), ("vec", 1)] + two(0, *order) + mixed + [("vec", 2)] + two(2, *order)
+        + [("three", 0), ("gather", 0), ("three", 1), ("gather", 1), ("vec", 3), ("store", 0), ("store", 1)]
+        + [("three", 2), ("gather", 2), ("store", 2)],
+        [],
+        [],
     )
 
 
@@ -55,9 +65,10 @@
         self.sent_rows = -(-CLUSTERS // 16) * 16
         self.small_rows = 8 if self.mates == 2 else 16
         self.count_rows = -(-self.heads // 8) * 8
-        self.tasks = schedule()
+        self.order = (0, 3, 1, 2)
+        self.tasks = schedule(self.order)
         self.square = (self.seq, self.block, self.width) if self.fast else (self.width, self.width)
-        self.y_first = ((True,) * 4, (False,) * 4, (True, False, True, False))
+        self.y_first = [[w[self.order.index(k)] for k in range(4)] for w in YF]
 
     def place(self, j):
         return lax.rem(j, self.rows), j // self.rows
@@ -450,7 +461,7 @@
         first_in = (f.first_in.at[0], f.first_in.at[1], f.w_down.at[2])
 
     def add(ref, value):
-        ref[...] = (ref[...].astype(F32) + value.astype(F32)).astype(BF16)
+        ref[...] = ref[...] + value
 
     def block(g, yp, xb, k):
         return core_in[g].at[yp, 2 * k + xb]
@@ -497,6 +508,7 @@
         step_one(g, k, other).wait_recv()
         add(own, first_in[g][other * deep + k])
         pl.when(far)(lambda: step_two(g, k).start())
+
 
     def step_three(g, k):
         return remote(
@@ -541,6 +553,14 @@
         gather_wait(g, 1)
         gather_copy(g, 2).start()
 
+    def store_copy(g):
+        return pltpu.make_async_copy(f.gat.at[g], f.sum_ref.at[g], f.load.at[g])
+
+    def store(g):
+        gather_wait(g, 0)
+        gather_wait(g, 2)
+        store_copy(g).start()
+
     def part_done(g, p):
         yp = p // 2
         part_core(g, p).wait_recv()
@@ -550,7 +570,7 @@
             return carry
 
         lax.fori_loop(0, z.seq, body, 0)
-        for k in range(deep):
+        for k in z.order:
             if y_first(g, k):
 
                 @pl.when(yp != y)
@@ -573,10 +593,6 @@
                     step_one(0, c, xx).start()
             else:
                 step_one(0, c, yp).start()
-
-    def core_done(c):
-        down_done(c)
-        pl.when(c % 2 == core)(lambda: part_done(1, c))
 
     def vec_copy(t, to):
         return remote(f.vec_buf.at[min(t, 2)], f.vec_got.at[t], f.v_ss.at[t], f.v_rs.at[t], to)
@@ -601,13 +617,16 @@
         if t == 3:
             f.vec_ref[...] = total
 
-    def part_step(which):
-        for p in range(2):
-            pl.when(core == p)(lambda p=p: part_done(2, p + which))
+    def part_step(p):
+        pl.when(core == p % 2)(lambda: part_done(2, p))
+
+    def up_step(c):
+        pl.when(c % 2 == core)(lambda: part_done(1, c))
 
     steps = {
+        "down": down_done, "store": store,
         "one": one_done, "two": two_done, "three": three_done, "gather": gather_done,
-        "vec": vec_step, "part": part_step,
+        "vec": vec_step, "part": part_step, "up": up_step,
     }
 
     def run(tasks):
@@ -641,23 +660,20 @@
     rows_sent(z, j, h, f.c_in, f.crow, f.c_send, f.c_recv)
     halves = z.rows // 2
 
-    def chunk(c, carry):
+    halves_of = [slice(t * halves, (t + 1) * halves) for t in range(2)]
+    rows_of = [slice(t * halves * part, (t + 1) * halves * part) for t in range(2)]
+
+    def ffn_chunk(c, carry):
         w_up, w_down = f.w_up[c].reshape(width, width), f.w_down[c].reshape(width, width)
         for t in range(2):
-            rows = slice(t * halves * part, (t + 1) * halves * part)
-            own = slice(t * halves, (t + 1) * halves)
-            grad_out = f.crow[own].reshape(halves * part, width)
+            rows, own = rows_of[t], halves_of[t]
             u = nn(f.low[rows, :], w_up)
             tanh = jnp.tanh(GELU_A * (u + GELU_B * (u * u * u)))
             cdf = 0.5 * (1.0 + tanh)
             f.act[own] = (u * cdf).astype(BF16).reshape(halves, part, width)
             slope = cdf + (0.5 * GELU_A) * u * (1.0 - tanh * tanh) * (1.0 + (3.0 * GELU_B) * (u * u))
-            grad = nt(grad_out, w_down)
-            f.gp[own] = (grad * slope).astype(BF16).reshape(halves, part, width)
+            f.slope[c, rows, :] = slope.astype(BF16)
             f.acc[rows, :] += nn(f.act[own].reshape(halves * part, width), w_down)
-            f.acc_n[rows, :] += nt(f.gp[own].reshape(halves * part, width), w_up)
-            if z.reduce and t == 0 and c:
-                core_done(c - 1)
         down = tn(
             f.act[...].reshape(z.tokens, width), f.crow[...].reshape(z.tokens, width)
         ).astype(BF16)
@@ -669,23 +685,44 @@
         else:
             f.d_down[pl.ds(pl.multiple_of(c * width, width), width), :] = down
         if z.reduce:
+            run(z.tasks[0][c])
             for yp in range(2):
                 down_core(yp, c).start()
+        return carry
+
+    def back_chunk(c, carry):
+        w_up, w_down = f.w_up[c].reshape(width, width), f.w_down[c].reshape(width, width)
+        for t in range(2):
+            rows, own = rows_of[t], halves_of[t]
+            grad = nt(f.crow[own].reshape(halves * part, width), w_down)
+            f.gp[own] = (grad * f.slope[c, rows, :].astype(F32)).astype(BF16).reshape(halves, part, width)
+            f.acc_n[rows, :] += nt(f.gp[own].reshape(halves * part, width), w_up)
         up = nn(f.low_t[...], f.gp[...].reshape(z.tokens, width)).astype(BF16)
         f.d_up[c] = up.reshape(f.d_up.shape[1:])
         if z.reduce:
+            run(z.tasks[1][c])
             pl.when(c % 2 != core)(lambda: part_core(1, c).start())
         return carry
 
-    if z.reduce:
-        for c in range(chunks):
-            chunk(c, 0)
-    else:
-        lax.fori_loop(0, chunks, chunk, 0)
+    def each_chunk(body, order):
+        if z.reduce:
+            for c in order:
+                body(c, 0)
+        else:
+            lax.fori_loop(0, chunks, body, 0)
+
+    each_chunk(ffn_chunk, z.order)
+
+    def ffn_out(t, carry):
+        f.act[t] = f.acc[part_rows(t), :].astype(BF16)
+        return carry
+
+    lax.fori_loop(0, z.rows, ffn_out, 0)
+    rows_out(z, j, r, h, f.act, f.out_ref, f.o_send, f.o_recv)
+    each_chunk(back_chunk, range(chunks))
 
     def ffn_back(t, carry):
         rows = part_rows(t)
-        f.act[t] = f.acc[rows, :].astype(BF16)
         unit, inverse = norm_parts(f.gm[rows, :])
         grad = f.acc_n[rows, :]
         grad_middle = f.crow[t].astype(F32) + norm_back(grad, unit, inverse, gain_ffn)
@@ -698,11 +735,10 @@
 
     zero = jnp.zeros((1, width), F32)
     sums_ffn = lax.fori_loop(0, z.rows, ffn_back, (zero, zero))
-    rows_out(z, j, r, h, f.act, f.out_ref, f.o_send, f.o_recv)
     f.ga_t[...] = nt(f.w_o[...], f.low[...]).astype(BF16)
 
     if z.reduce:
-        core_done(chunks - 1)
+        run(z.tasks[2])
 
     def gather_grads(i, carry):
         blocks = []
@@ -715,7 +751,7 @@
             f.g_send[i, d] = packed
         for step in others:
             grad_copy(i, step).start()
-        serve(i, z.tasks[0])
+        serve(i, z.tasks[3])
         return carry
 
     lax.fori_loop(0, pairs, gather_grads, 0)
@@ -724,7 +760,7 @@
         pl.when(core == 0)(lambda: part_core(2, 3).start())
 
     def attend_back(i, carry):
-        serve(i, z.tasks[1])
+        serve(i, z.tasks[4])
         got = []
         for step in others:
             grad_copy(i, step).wait()
@@ -769,6 +805,8 @@
         return carry
 
     lax.fori_loop(0, pairs, attend_back, 0)
+    if z.reduce:
+        run(z.tasks[8])
 
     def weight_grad(p, g_ref):
         f.w_up[p] = nt(f.n_t[...], g_ref[...]).astype(BF16).reshape(z.square)
@@ -787,14 +825,16 @@
             n = 2 * i + a
             low = (total[a * z.head : (a + 1) * z.head] / f.cnts[pl.ds(n, 1), :]).astype(BF16)
             f.q_t[head_rows(n), :] = nn(low, member_of(n)).astype(BF16)
-        serve(i, z.tasks[2])
+        serve(i, z.tasks[5])
         return carry
 
     lax.fori_loop(0, pairs, query_back, 0)
+    if z.reduce:
+        run(z.tasks[9])
     weight_grad(0, f.q_t)
 
     if z.reduce:
-        run(z.tasks[3])
+        run(z.tasks[6])
 
     total = (
         nn(f.w_qkv[0], f.q_t[...]) + nn(f.w_qkv[1], f.gk_t[...]) + nn(f.w_qkv[2], f.gv_t[...])
@@ -818,20 +858,16 @@
     if z.reduce:
         f.vec_buf[0] = vectors
         vec_copy(0, {"dp": sibling}).start()
-        run(z.tasks[4])
+        run(z.tasks[7])
         for g in range(3):
-            gather_wait(g, 0)
-            gather_wait(g, 2)
+            store_copy(g).wait()
             for kind in range(3):
                 gather_copy(g, kind).wait_send()
             for k in range(deep):
                 for other in range(2):
                     step_one(g, k, other).wait_send()
                 step_two(g, k).wait_send()
-
-                @pl.when(zz != k)
-                def _():
-                    step_three(g, k).wait_send()
+                pl.when(zz != k)(lambda k=k, g=g: step_three(g, k).wait_send())
 
         for yp in range(2):
             for c in range(chunks):
@@ -850,6 +886,44 @@
         rows_landed(z, j, h, f.gp, f.gx_ref, f.y_send, f.y_recv, slot)
     rows_sent(z, j, h, f.act, f.out_ref, f.o_send, f.o_recv)
     rows_sent(z, j, h, f.gp, f.gx_ref, f.y_send, f.y_recv)
+
+
+def publish_kernel(
+    z, rows_a, rows_b, sums, vectors, out_a, out_b, w_q, w_k, w_v, w_o, w_up, w_down, own,
+    rows_in, sums_in, rows_wide, sums_wide, r_in, r_out, s_in, s_out,
+):
+    pieces = []
+    for a, (src, dst) in enumerate(((rows_a, out_a), (rows_b, out_b))):
+        for t in range(z.rows):
+            pieces.append(
+                (src.at[t], rows_in.at[a, t], rows_wide.at[a, t], dst.at[t], r_in.at[a, t], r_out.at[a, t])
+            )
+    for g in range(3):
+        for p in range(z.dp):
+            if g == 0:
+                dst = w_down.at[pl.ds(p * z.block, z.block), :]
+            elif g == 1:
+                dst = w_up.at[:, pl.ds(p * z.width, z.width)]
+            else:
+                dst = (w_q, w_k, w_v, w_o)[p]
+            pieces.append(
+                (sums.at[g, p], sums_in.at[g, p], sums_wide.at[g, p], dst, s_in.at[g, p], s_out.at[g, p])
+            )
+    for src, low, _, _, sem, _ in pieces:
+        pltpu.make_async_copy(src, low, sem).start()
+    for src, low, wide, dst, sem, done in pieces:
+        pltpu.make_async_copy(src, low, sem).wait()
+        wide[...] = low[...].astype(F32)
+        pltpu.make_async_copy(wide, dst, done).start()
+    first = lax.axis_index("seq") * z.block
+    rows = lax.broadcasted_iota(jnp.int32, (z.width, PAD), 0)
+    lanes = lax.broadcasted_iota(jnp.int32, (z.width, PAD), 1)
+    pick = jnp.where(rows == lanes + first, 1.0, 0.0)
+    own[...] = jnp.dot(
+        vectors[...], pick, precision=lax.Precision.HIGHEST, preferred_element_type=F32
+    )
+    for _, _, wide, dst, _, done in pieces:
+        pltpu.make_async_copy(wide, dst, done).wait()
 
 
 def local(
@@ -904,6 +978,7 @@
         ("c_got", (others, pairs) + packed, BF16),
         ("low", (tokens, width), BF16), ("low_t", (width, tokens), BF16),
         ("act", rows, BF16), ("gp", rows, BF16),
+        ("slope", (chunks, tokens, width), BF16),
         ("acc", (tokens, width), F32), ("acc_n", (tokens, width), F32), ("gm", (tokens, width), F32),
         ("ga_t", (width, tokens), BF16), ("gk_t", (width, tokens), BF16), ("gv_t", (width, tokens), BF16),
     ]
@@ -916,8 +991,9 @@
     if z.fast:
         piece = (z.block, width)
         deep = z.seq // 2
-        outs.append(("gat", shape((3, z.dp) + piece, BF16), vmem))
+        outs.append(("sum_ref", shape((3, z.dp) + piece, BF16), anywhere))
         scratch += [
+            ("gat", (3, z.dp) + piece, BF16),
             ("d_down", (z.dp, z.seq) + piece, BF16), ("d_up", (z.dp, z.seq) + piece, BF16),
             ("core_in", (2, 2, z.seq) + piece, BF16), ("first_in", (2, z.seq) + piece, BF16),
             ("second_in", (3, deep) + piece, BF16), ("third_in", (3, deep) + piece, BF16),
@@ -949,19 +1025,36 @@
 
     out_back, grad_back, vectors = results[:3]
     if z.fast:
-        gat = results[3].astype(F32)
-        g_down = gat[0].reshape(-1, width)
-        g_up = jnp.transpose(gat[1], (1, 0, 2)).reshape(z.block, -1)
-        g_qkvo = gat[2]
-        own = lax.dynamic_slice_in_dim(vectors, lax.axis_index("seq") * z.block, z.block, 1)
-    else:
-
-        def share(v, dim):
-            v = lax.psum_scatter(v.astype(F32), "seq", scatter_dimension=dim, tiled=True)
-            return lax.psum(v, "dp")
-
-        g_up = share(jnp.transpose(results[4], (1, 0, 2)).reshape(width, z.hidden), 0)
-        g_qkvo, g_down, own = share(results[3], 1), share(results[5], 0), share(vectors, 1)
+        flat = shape((z.block, width), F32)
+        grid_rows = (z.rows, z.part, width)
+        published = pl.pallas_call(
+            functools.partial(publish_kernel, z),
+            out_shape=[
+                shape(grid_rows, F32), shape(grid_rows, F32), flat, flat, flat, flat,
+                shape((z.block, z.hidden), F32), shape((z.hidden // z.seq, width), F32),
+                shape((8, PAD), F32),
+            ],
+            in_specs=[anywhere] * 3 + [vmem],
+            out_specs=[anywhere] * 8 + [vmem],
+            scratch_shapes=[
+                pltpu.VMEM((2,) + grid_rows, BF16), pltpu.VMEM((3, z.dp) + piece, BF16),
+                pltpu.VMEM((2,) + grid_rows, F32), pltpu.VMEM((3, z.dp) + piece, F32),
+                dma((2, z.rows)), dma((2, z.rows)), dma((3, z.dp)), dma((3, z.dp)),
+            ],
+            compiler_params=pltpu.CompilerParams(vmem_limit_bytes=VMEM_LIMIT),
+        )(out_back, grad_back, results[3], vectors)
+        out_full, grad_full, g_q, g_k, g_v, g_o, g_up, g_down, own = published
+        own = own[:, : z.block]
+        return (
+            out_full, grad_full, own[0], own[1], g_q, g_k, g_v, g_o, own[2], own[3], g_up, g_down,
+        )
+
+    def share(v, dim):
+        v = lax.psum_scatter(v.astype(F32), "seq", scatter_dimension=dim, tiled=True)
+        return lax.psum(v, "dp")
+
+    g_up = share(jnp.transpose(results[4], (1, 0, 2)).reshape(width, z.hidden), 0)
+    g_qkvo, g_down, own = share(results[3], 1), share(results[5], 0), share(vectors, 1)
     return (
         out_back.astype(F32), grad_back.astype(F32), own[0], own[1],
         g_qkvo[0], g_qkvo[1], g_qkvo[2], g_qkvo[3], own[2], own[3], g_up, g_down,

time: 158 us -> 149 us (0.943)
  the two profiles are of different devices: /device:TPU:25 before, /device:TPU:0 now
where the time goes in v3:
time: 149 us; the launch traced here: 146 us
  Pallas kernels  144 us (97%)
    pallas_call x1, Pallas kernels, local(): pl.pallas_call(functools.partial(block_kernel, z, names), out_shape=[s fo...  139 us
    pallas_call x1, Pallas kernels, local(): pl.pallas_call(functools.partial(publish_kernel, z), out_shape=[shape(gri...  5.68 us

profile of v3, /device:TPU:0, one launch (start us, length us, event | category | flops | bytes accessed | tf_op | source)
XLA Modules:
  0.0 146.5 jit_solution(4597690081469453434)
XLA Ops:
  0.6 138.8 %shard_map.229 = (bf16[4,128,768]{2,1,0:T(8,128)(2,1)}, bf16[4,128,768]{2,1,0:T(8,128)(2,1)}, f32[8,768]{1,0:T(8,128)}, bf16[3,4,96,768]{3,2,1,0:T(8,128)(2,1)}) custom-call(bf16[4,128,768]{2,1,0:T(8,128)(2,1)} %values_0_.1, bf16[4,128,768]{2,1,0:T(8,128)(2,1)} %values_1_.1, s32[12,4,128]{2,1,0:T(4,128)} %bitcast.13, s32[4,4]{1,0:T(4,128)} %values_3_.1, ...), custom_call_target="tpu_custom_call" | custom-call | tf_op jit(solution)/shard_map/pallas_call | solution.py:1015
  139.4 5.7 %shard_map.230 = (f32[4,128,768]{2,1,0:T(8,128)}, f32[4,128,768]{2,1,0:T(8,128)}, f32[96,768]{1,0:T(8,128)}, f32[96,768]{1,0:T(8,128)}, f32[96,768]{1,0:T(8,128)...) custom-call(bf16[4,128,768]{2,1,0:T(8,128)(2,1)} %get-tuple-element.25.rows_a, ...), custom_call_target="tpu_custom_call" | custom-call | tf_op jit(solution)/shard_map/pallas_call | solution.py:1030
  145.1 1.3 slice_bitcast_fusion

commit v4 on v3

--- a/solution.py
+++ b/solution.py
@@ -41,8 +41,8 @@
         ((),) * 6,
         both(1, *order),
         [("part", 3), ("part", 1), ("part", 2), ("part", 0), ("vec", 1)] + two(0, *order) + mixed + [("vec", 2)] + two(2, *order)
-        + [("three", 0), ("gather", 0), ("three", 1), ("gather", 1), ("vec", 3), ("store", 0), ("store", 1)]
-        + [("three", 2), ("gather", 2), ("store", 2)],
+        + [("three", 0), ("gather", 0), ("three", 1), ("gather", 1), ("three", 2), ("vec", 3), ("store", 0)]
+        + [("store", 1), ("gather", 2), ("store", 2)],
         [],
         [],
     )
@@ -643,18 +643,20 @@
         copy.wait()
 
     def first(t, carry):
-        rows = part_rows(t)
-        middle = f.xrow[t].astype(F32) + tn(f.att_t[:, rows], f.w_o[...])
+        size = 2 * part
+        rows = pl.ds(pl.multiple_of(t * size, size), size)
+        values = f.xrow[pl.ds(2 * t, 2)].reshape(size, width).astype(F32)
+        middle = values + tn(f.att_t[:, rows], f.w_o[...])
         f.acc[rows, :] = middle
         f.gm[rows, :] = middle
         unit, _ = norm_parts(middle)
         normed = (unit * gain_ffn + bias_ffn).astype(BF16)
         f.low[rows, :] = normed
         f.low_t[:, rows] = normed.T
-        f.acc_n[rows, :] = jnp.zeros((part, width), F32)
-        return carry
-
-    lax.fori_loop(0, z.rows, first, 0)
+        f.acc_n[rows, :] = jnp.zeros((size, width), F32)
+        return carry
+
+    lax.fori_loop(0, z.rows // 2, first, 0)
     for slot in range(z.rows):
         rows_landed(z, j, h, f.c_in, f.crow, f.c_send, f.c_recv, slot)
     rows_sent(z, j, h, f.c_in, f.crow, f.c_send, f.c_recv)

time: 149 us -> 148 us (level)
  no operation moved by 1% of the time
where the time goes in v4:
time: 148 us; the launch traced here: 146 us
  Pallas kernels  143 us (97%)
    pallas_call x1, Pallas kernels, local(): pl.pallas_call(functools.partial(block_kernel, z, names), out_shape=[s fo...  138 us
    pallas_call x1, Pallas kernels, local(): pl.pallas_call(functools.partial(publish_kernel, z), out_shape=[shape(gri...  5.68 us

profile of v4, /device:TPU:0, one launch (start us, length us, event | category | flops | bytes accessed | tf_op | source)
XLA Modules:
  0.0 145.5 jit_solution(13504876052095851740)
XLA Ops:
  0.6 137.8 %shard_map.229 = (bf16[4,128,768]{2,1,0:T(8,128)(2,1)}, bf16[4,128,768]{2,1,0:T(8,128)(2,1)}, f32[8,768]{1,0:T(8,128)}, bf16[3,4,96,768]{3,2,1,0:T(8,128)(2,1)}) custom-call(bf16[4,128,768]{2,1,0:T(8,128)(2,1)} %values_0_.1, bf16[4,128,768]{2,1,0:T(8,128)(2,1)} %values_1_.1, s32[12,4,128]{2,1,0:T(4,128)} %bitcast.13, s32[4,4]{1,0:T(4,128)} %values_3_.1, ...), custom_call_target="tpu_custom_call" | custom-call | tf_op jit(solution)/shard_map/pallas_call | solution.py:1017
  138.5 5.7 %shard_map.230 = (f32[4,128,768]{2,1,0:T(8,128)}, f32[4,128,768]{2,1,0:T(8,128)}, f32[96,768]{1,0:T(8,128)}, f32[96,768]{1,0:T(8,128)}, f32[96,768]{1,0:T(8,128)...) custom-call(bf16[4,128,768]{2,1,0:T(8,128)(2,1)} %get-tuple-element.25.rows_a, ...), custom_call_target="tpu_custom_call" | custom-call | tf_op jit(solution)/shard_map/pallas_call | solution.py:1032
  144.2 1.3 slice_bitcast_fusion

commit v5 on v4

--- a/solution.py
+++ b/solution.py
@@ -349,12 +349,13 @@
     f.cnts[...] = jnp.maximum(counts, 1.0)
 
     def project_more(t, carry):
-        normed = f.low[part_rows(t), :]
-        f.k_t[:, part_rows(t)] = nn(normed, f.w_qkv[1]).astype(BF16).T
-        f.v_t[:, part_rows(t)] = nn(normed, f.w_qkv[2]).astype(BF16).T
-        return carry
-
-    lax.fori_loop(0, z.rows, project_more, 0)
+        rows = pl.ds(pl.multiple_of(t * 2 * part, 2 * part), 2 * part)
+        normed = f.low[rows, :]
+        f.k_t[:, rows] = nn(normed, f.w_qkv[1]).astype(BF16).T
+        f.v_t[:, rows] = nn(normed, f.w_qkv[2]).astype(BF16).T
+        return carry
+
+    lax.fori_loop(0, z.rows // 2, project_more, 0)
 
     def masked_values(i):
         return jnp.concatenate([f.v_t[head_rows(i), :]] * z.docs, axis=0) * f.body[...]

time: 148 us -> 148 us (level)
  no operation moved by 1% of the time
where the time goes in v5:
time: 148 us; the launch traced here: 145 us
  Pallas kernels  143 us (97%)
    pallas_call x1, Pallas kernels, local(): pl.pallas_call(functools.partial(block_kernel, z, names), out_shape=[s fo...  138 us
    pallas_call x1, Pallas kernels, local(): pl.pallas_call(functools.partial(publish_kernel, z), out_shape=[shape(gri...  5.68 us

profile of v5, /device:TPU:0, one launch (start us, length us, event | category | flops | bytes accessed | tf_op | source)
XLA Modules:
  0.0 145.5 jit_solution(15181775417030219927)
XLA Ops:
  0.6 137.8 %shard_map.229 = (bf16[4,128,768]{2,1,0:T(8,128)(2,1)}, bf16[4,128,768]{2,1,0:T(8,128)(2,1)}, f32[8,768]{1,0:T(8,128)}, bf16[3,4,96,768]{3,2,1,0:T(8,128)(2,1)}) custom-call(bf16[4,128,768]{2,1,0:T(8,128)(2,1)} %values_0_.1, bf16[4,128,768]{2,1,0:T(8,128)(2,1)} %values_1_.1, s32[12,4,128]{2,1,0:T(4,128)} %bitcast.13, s32[4,4]{1,0:T(4,128)} %values_3_.1, ...), custom_call_target="tpu_custom_call" | custom-call | tf_op jit(solution)/shard_map/pallas_call | solution.py:1018
  138.5 5.7 %shard_map.230 = (f32[4,128,768]{2,1,0:T(8,128)}, f32[4,128,768]{2,1,0:T(8,128)}, f32[96,768]{1,0:T(8,128)}, f32[96,768]{1,0:T(8,128)}, f32[96,768]{1,0:T(8,128)...) custom-call(bf16[4,128,768]{2,1,0:T(8,128)(2,1)} %get-tuple-element.25.rows_a, ...), custom_call_target="tpu_custom_call" | custom-call | tf_op jit(solution)/shard_map/pallas_call | solution.py:1033
  144.1 1.3 slice_bitcast_fusion
